TPU v7x, 512 devices: a whole 4x8x8 slice. The times are simulated.
512 devices in a mesh: cand: 16 (over z, core), fsdp: 16 (over x_hi, y), prompt: 2 (over x_lo).
Axes of the slice: x: 4 (x_hi: 2, x_lo: 2; x = x_hi * 2 + x_lo), y: 8, z: 8, core: 2. Of those that a mesh axis runs over, the one named last changes fastest.
Arguments:
- hidden: bfloat16 [2, 16, 8192, 4608], P('prompt', 'cand', 'fsdp'), may hold values from -12 to 12
- lengths: int32 [2, 16], P('prompt', 'cand'), may hold values from 2048 to 8192, as said below
- starts: int32 [2, 16], P('prompt', 'cand'), may hold values from 0 to 1023
- ranking: int32 [2, 16], P('prompt'), may hold values from 0 to 15, each once within a row
- down_w: bfloat16 [96, 4608], P(None, 'fsdp'), may hold values from -0.09375 to 0.09375
- up_w: bfloat16 [96, 4608], P(None, 'fsdp'), may hold values from -0.625 to 0.625
- gain: bfloat16 [4608], P('fsdp'), may hold values from 0.5 to 1.5
- head: bfloat16 [4608], P('fsdp'), may hold values from -1 to 1
Outputs:
- list_loss: float32 [2], P('prompt')
- down_grad: float32 [96, 4608], P(None, 'fsdp')
- up_grad: float32 [96, 4608], P(None, 'fsdp')
- gain_grad: float32 [4608], P('fsdp')
- head_grad: float32 [4608], P('fsdp')
Inputs may be any that keep to these rules, and one draw needn't show every extreme that they name: `lengths`: every prompt has a candidate of length 8192.
All inputs are finite; a program needn't handle non-finite values.
Results may differ from a plain program's by a relative error of at most 0.0003.
Values may be sent and summed in bfloat16 or wider, within the bound.
No kernel may reach another device: no remote copies, remote signals or barrier semaphores. Data moves between devices by JAX's collectives and lax.ppermute only.
A program may use at most 64 MiB of HBM per device.

v0:
```python
import jax
import jax.numpy as jnp
from jax import lax
from jax.sharding import PartitionSpec as P

loss_scale = 256.0


def token_forward(rows, down_full, up_full, gain_f, head_f):
    pre = lax.dot_general(
        rows, down_full, (((1,), (1,)), ((), ())), preferred_element_type=jnp.float32
    )
    act = jax.nn.silu(pre).astype(jnp.bfloat16)
    mixed = rows.astype(jnp.float32) + jnp.dot(act, up_full, preferred_element_type=jnp.float32)
    inv = lax.rsqrt(jnp.mean(mixed * mixed, axis=-1, keepdims=True) + 1e-06)
    scaled = mixed * inv
    score = jnp.sum(scaled * (gain_f * head_f)[None, :], axis=-1)
    return (pre, act, scaled, inv, score)


def token_backward(rows, up_full, gain_f, head_f, pre, act, scaled, inv, weight):
    pooled = jnp.dot(weight, scaled, precision=lax.Precision.HIGHEST)
    head_grad = gain_f * pooled
    gain_grad = head_f * pooled
    upper = weight[:, None] * (head_f * gain_f)[None, :]
    mixed_grad = (inv * (upper - scaled * jnp.mean(upper * scaled, axis=-1, keepdims=True))).astype(
        jnp.bfloat16
    )
    up_grad = lax.dot_general(
        act, mixed_grad, (((0,), (0,)), ((), ())), preferred_element_type=jnp.float32
    )
    back = lax.dot_general(
        mixed_grad, up_full, (((1,), (1,)), ((), ())), preferred_element_type=jnp.float32
    )
    sigma = jax.nn.sigmoid(pre)
    pre_grad = (back * sigma * (1.0 + pre * (1.0 - sigma))).astype(jnp.bfloat16)
    down_grad = lax.dot_general(
        pre_grad, rows, (((0,), (0,)), ((), ())), preferred_element_type=jnp.float32
    )
    return (down_grad, up_grad, gain_grad, head_grad)


def ranked_loss(rewards, order):
    ranked = jnp.take(rewards, order)
    width = ranked.shape[0]
    index = lax.iota(jnp.int32, width)
    later = index[None, :] >= index[:, None]
    top = lax.stop_gradient(jnp.max(jnp.where(later, ranked[None, :], -1e30), axis=1))
    diff = jnp.where(later, ranked[None, :] - top[:, None], -10000.0)
    return jnp.sum(top + jnp.log(jnp.sum(jnp.exp(diff), axis=1)) - ranked)


def on_device(hidden, lengths, starts, ranking, down_w, up_w, gain, head):
    rows = hidden[0, 0]
    tokens = rows.shape[0]
    down_full, up_full, gain_full, head_full = (
        lax.all_gather(down_w, "fsdp", axis=1, tiled=True),
        lax.all_gather(up_w, "fsdp", axis=1, tiled=True),
        lax.all_gather(gain, "fsdp", axis=0, tiled=True),
        lax.all_gather(head, "fsdp", axis=0, tiled=True),
    )
    gain_f = gain_full.astype(jnp.float32)
    head_f = head_full.astype(jnp.float32)
    pre, act, scaled, inv, score = token_forward(rows, down_full, up_full, gain_f, head_f)
    positions = lax.axis_index("fsdp") * tokens + lax.iota(jnp.int32, tokens)
    length = lengths[0, 0]
    start = starts[0, 0]
    valid = (positions >= start) & (positions < length)
    count = (length - start).astype(jnp.float32)
    partial_value = jnp.sum(jnp.where(valid, score, 0.0)) / count
    mine = lax.axis_index("cand")
    reward = lax.psum(partial_value, "fsdp")
    rewards = lax.all_gather(reward.reshape(1), "cand", axis=0, tiled=True)
    order = ranking[0]
    loss, pull = jax.vjp(lambda v: ranked_loss(v, order), rewards)
    slopes = pull(jnp.ones_like(loss))[0]
    slope = lax.dynamic_slice_in_dim(slopes, mine, 1)[0]
    weight = jnp.where(valid, loss_scale * slope / count, 0.0)
    terms = token_backward(rows, up_full, gain_f, head_f, pre, act, scaled, inv, weight)
    totals = lax.psum((terms[0], terms[1], terms[2], terms[3]), ("cand", "prompt"))
    grads = (
        lax.psum_scatter(totals[0], "fsdp", scatter_dimension=1, tiled=True),
        lax.psum_scatter(totals[1], "fsdp", scatter_dimension=1, tiled=True),
        lax.psum_scatter(totals[2], "fsdp", scatter_dimension=0, tiled=True),
        lax.psum_scatter(totals[3], "fsdp", scatter_dimension=0, tiled=True),
    )
    return (loss.reshape(1), grads[0], grads[1], grads[2], grads[3])


def solution(mesh):
    placed = (
        P("prompt", "cand", "fsdp", None),
        P("prompt", "cand"),
        P("prompt", "cand"),
        P("prompt", None),
        P(None, "fsdp"),
        P(None, "fsdp"),
        P("fsdp"),
        P("fsdp"),
    )
    return jax.shard_map(
        on_device,
        mesh=mesh,
        in_specs=placed,
        out_specs=(P("prompt"), P(None, "fsdp"), P(None, "fsdp"), P("fsdp"), P("fsdp")),
        check_vma=False,
    )
```

profile of v0, /device:TPU:1, one launch (start us, length us, event | category | flops | bytes accessed | tf_op | source)
XLA Modules:
  0.0 945.2 jit_solution(1094156493636960866)
XLA Ops:
  7.2 1.0 copy.15
  8.2 43.0 %all_gather.15 = bf16[96,4608]{0,1:T(8,128)(2,1)S(1)} all-gather(bf16[96,288]{0,1:T(8,128)(2,1)S(1)} %copy.15), channel_id=1, replica_groups=mesh['cand'=16,'fsdp'=16,'prompt'=2] {'fsdp'}, dimensions={1}, use_global_device_ids=true | all-gather | bytes 940032 | tf_op jit(solution)/shard_map/all_gather | solution.py:57
  51.2 1.0 copy.16
  52.2 37.1 %all_gather.16 = bf16[96,4608]{0,1:T(8,128)(2,1)S(1)} all-gather(bf16[96,288]{0,1:T(8,128)(2,1)S(1)} %copy.16), channel_id=1, replica_groups=mesh['cand'=16,'fsdp'=16,'prompt'=2] {'fsdp'}, dimensions={1}, use_global_device_ids=true | all-gather | bytes 940032 | tf_op jit(solution)/shard_map/all_gather | solution.py:58
  89.3 4.0 fusion.6
  93.4 5.2 multiply_reduce_fusion.1
  101.7 59.2 %all-reduce.8 = (bf16[4608]{0:T(1024)(128)(2,1)S(1)}, bf16[4608]{0:T(1024)(128)(2,1)S(1)}) all-reduce(bf16[4608]{0:T(1024)(128)(2,1)S(1)} %dynamic-update-slice.1, bf16[4608]{0:T(1024)(128)(2,1)S(1)} %dynamic-update-slice), channel_id=1, replica_groups=mesh['cand'=16,'fsdp'=16,'prompt'=2] {'fsdp'}, use_global_device_ids=true, to_apply=%add.1 | all-reduce | flops 9216 | bytes 36864
  160.9 4.8 multiply_reduce_fusion
  165.7 0.6 select_reduce_fusion.2
  167.0 30.8 %psum.35 = f32[1]{0:T(128)} all-reduce(f32[1]{0:T(128)} %bitcast.4), channel_id=1, replica_groups=mesh['cand'=16,'fsdp'=16,'prompt'=2] {'fsdp'}, use_global_device_ids=true, to_apply=%region_3.4 | all-reduce | flops 1 | bytes 8 | tf_op jit(solution)/shard_map/psum | solution.py:72
  197.8 1.3 dynamic-slice.2
  199.1 1.4 dynamic-update-slice.2
  200.5 64.1 %all-reduce.2 = f32[16]{0:T(128)S(1)} all-reduce(f32[16]{0:T(128)S(1)} %dynamic-update-slice.2), channel_id=1, replica_groups=mesh['cand'=16,'fsdp'=16,'prompt'=2] {'cand'}, use_global_device_ids=true, to_apply=%add.2 | all-reduce | flops 16 | bytes 128
  264.6 0.7 gather_fusion
  265.6 0.6 broadcast_divide_fusion
  266.3 0.7 scatter_custom_fusion
  268.3 5.3 fusion
  273.6 1.0 copy-done
  274.6 2.9 fusion.2
  277.6 2.2 copy-done.1
  279.8 3.4 convolution_bitcast_fusion
  283.5 8.1 convolution_bitcast_fusion.1
  292.3 7.5 fusion.11
  299.8 188.3 %reduce-scatter.9.cloned.1.call-done = f32[288,96]{1,0:T(8,128)} async-done(((f32[4608,96]{1,0:T(8,128)}), f32[288,96]{1,0:T(8,128)}) %reduce-scatter.9.cloned.1.call-update) | async-done | bytes 110608
  488.1 1.7 copy.20
  489.8 218.3 %reduce-scatter.7.cloned.1.call-done = f32[288,96]{1,0:T(8,128)} async-done(((f32[4608,96]{1,0:T(8,128)}), f32[288,96]{1,0:T(8,128)}) %reduce-scatter.7.cloned.1.call-update) | async-done | bytes 110608
  708.1 1.7 copy.18
  709.8 60.3 %all-reduce.7 = (f32[4608]{0:T(1024)S(1)}, f32[4608]{0:T(1024)S(1)}) all-reduce(f32[4608]{0:T(1024)S(1)} %get-tuple-element.14, f32[4608]{0:T(1024)S(1)} %get-tuple-element.13), channel_id=4, replica_groups=mesh['cand'=16,'fsdp'=16,'prompt'=2] {'fsdp'}, use_global_device_ids=true, to_apply=%region_15.16.clone | all-reduce | flops 9216 | bytes 73728
  770.3 71.4 %all-reduce.5 = (f32[288]{0:T(512)}, f32[288]{0:T(512)}) all-reduce(f32[288]{0:T(512)S(1)} %dynamic-slice.4, f32[288]{0:T(512)S(1)} %dynamic-slice.6), channel_id=1, replica_groups=mesh['cand'=16,'fsdp'=16,'prompt'=2] {'cand','prompt'}, use_global_device_ids=true, to_apply=%region_14.15 | all-reduce | flops 576 | bytes 4608 | tf_op jit(solution)/shard_map/psum | solution.py:80
  841.7 93.8 %all-reduce.11.cloned.1.call-done = (f32[96,288]{1,0:T(8,128)}, f32[96,288]{1,0:T(8,128)}) async-done(((f32[96,288]{1,0:T(8,128)}, f32[96,288]{1,0:T(8,128)}), (f32[96,288]{1,0:T(8,128)}, f32[96,288]{1,0:T(8,128)})) %all-reduce.11.cloned.1.call-update) | async-done | bytes 221200 | tf_op jit(solution)/shard_map/psum | solution.py:80
  935.5 1.6 copy.28
  937.1 1.6 copy.29
  (42 shorter events, 2.7 us)
Async XLA Ops:
  7.2 481.0 %reduce-scatter.9.cloned.1.call-start = ((), (), s32[]{:S(2)}) async-start(), calls=%async_computation.3 | async-start | bytes 2506752
  52.2 41.1 %slice-start = ((s8[4718592]{0:T(1024)(128)(4,1)}), s8[4194304]{0:T(1024)(128)(4,1)S(1)}, s32[]{:S(2)}) async-start(s8[4718592]{0:T(1024)(128)(4,1)} %bitcast.47), calls=%async_computation.5 | async-start | bytes 8388608
  89.3 4.0 slice-start.1
  93.4 6.5 copy-start.4
  93.4 7.8 copy-start.2
  93.4 8.0 copy-start.3
  160.9 103.7 %copy-start.5 = (s32[1,16]{1,0:T(1,128)S(1)}, s32[1,16]{1,0:T(1,128)}, u32[]{:S(2)}) copy-start(s32[1,16]{1,0:T(1,128)} %param.11) | copy-start | bytes 196
  268.3 6.4 copy-start
  277.6 2.2 copy-start.1
  283.2 424.9 %reduce-scatter.7.cloned.1.call-start = ((), (), s32[]{:S(2)}) async-start(), calls=%async_computation.2 | async-start | bytes 2506752
  291.6 643.9 %all-reduce.11.cloned.1.call-start = ((), (), s32[]{:S(2)}) async-start(), calls=%async_computation.4 | async-start | bytes 589824 | tf_op jit(solution)/shard_map/psum | solution.py:80
Sparse Core Ops, SparseCore 0:
  283.4 204.7 reduce-scatter.8
  492.7 215.3 reduce-scatter.6
  711.7 223.8 all-reduce.10
where the time goes:
time: 946 us; the launch traced here: 945 us
  waiting for transfers between devices  500 us (53%)
  blocking collectives  366 us (39%)
  matrix products  28.2 us (3%)
  between operations  17.9 us (2%)
  local copies, waits for them, and re-layouts  17 us (2%)
  other arithmetic  15.4 us (2%)
    unnamed x5, waiting for transfers between devices  407 us
    unnamed x3, blocking collectives  184 us
    psum x1, waiting for transfers between devices, on_device(): lax.psum((terms[0], terms[1], terms[2], terms[3]), ('cand', 'prompt'))  93.8 us
    psum x1, blocking collectives, on_device(): lax.psum((terms[0], terms[1], terms[2], terms[3]), ('cand', 'prompt'))  71.4 us
    all_gather x1, blocking collectives, on_device(): lax.all_gather(down_w, 'fsdp', axis=1, tiled=True)  43 us
    all_gather x1, blocking collectives, on_device(): lax.all_gather(up_w, 'fsdp', axis=1, tiled=True)  37.1 us
    psum x1, blocking collectives, on_device(): reward = lax.psum(partial_value, 'fsdp')  30.8 us
  transfers between devices with their start and end apart: 3, of which 3 were waited for; matrix products, arithmetic and copies ran while one was open for 2% of the time, Pallas kernels for 0%

commit v1 on v0

v1 whole, which is shorter than its diff:
```python
import functools

import jax
import jax.numpy as jnp
from jax import lax
from jax.experimental import pallas as pl
from jax.experimental.pallas import tpu as pltpu
from jax.sharding import PartitionSpec as P

loss_scale = 256.0
D = 4608
R = 96
TOK = 512
NB = 16
BW = 288
CH = 512
STEPS = 32760.0
FINE = 60000.0
TINY = 1e-36
f32 = jnp.float32
bf16 = jnp.bfloat16
VMEM = pl.BlockSpec(memory_space=pltpu.VMEM)
SMEM = pl.BlockSpec(memory_space=pltpu.SMEM)


def mm(a, b, ca, cb):
    return lax.dot_general(a, b, (((ca,), (cb,)), ((), ())), preferred_element_type=f32)


def halves(v):
    hi = v.astype(bf16)
    return hi, (v - hi.astype(f32)).astype(bf16)


def lanes(shape):
    return lax.broadcasted_iota(jnp.int32, shape, len(shape) - 1)


def level(most):
    return jnp.ceil(jnp.log2(jnp.maximum(most, TINY)) * 8.0)


def coded(v, e):
    return jnp.round(v * jnp.exp2(e * -0.125) * STEPS).astype(jnp.int32)


def local_kernel(info, x_ref, mine_ref, other_ref, out_ref, w_ref, ss_ref, g_ref, p_ref):
    start, length, first, core = info[0], info[1], info[2], info[3]

    @pl.when(core == 0)
    def _():
        w_ref[:, :128] = mine_ref[...]
        w_ref[:, 128:] = other_ref[...]

    @pl.when(core != 0)
    def _():
        w_ref[:, :128] = other_ref[...]
        w_ref[:, 128:] = mine_ref[...]

    def square(i, carry):
        rows = x_ref[pl.ds(pl.multiple_of(i * 16, 16), 16), :].astype(f32)
        ss_ref[pl.ds(pl.multiple_of(i * 16, 16), 16), :] = jnp.sum(rows * rows, axis=1, keepdims=True)
        return carry

    lax.fori_loop(0, TOK // 16, square, 0)

    prod = mm(x_ref[...], w_ref[...], 1, 0)
    gram = mm(w_ref[...], w_ref[...], 0, 0)
    pre = prod[:, :128]
    x_up = prod[:, 128:]
    lane = lanes((TOK, 128))
    unit = lane < R
    sig = 1.0 / (1.0 + jnp.exp(-pre))
    act_b = jnp.where(unit, pre * sig, 0.0).astype(bf16)
    act = act_b.astype(f32)
    g_hi, g_lo = halves(gram[128:, :])
    through = mm(act_b, g_hi, 1, 0) + mm(act_b, g_lo, 1, 0)
    m_left = pre + through[:, :128]
    m_up = x_up + through[:, 128:]
    m_head = jnp.sum(jnp.where((lane == R) | (lane == R + 1), m_left, 0.0), axis=1, keepdims=True)
    m_sq = ss_ref[...] + jnp.sum(act * (x_up + m_up), axis=1, keepdims=True)
    inv = lax.rsqrt(jnp.maximum(m_sq, 0.0) * (1.0 / D) + 1e-06)
    score = inv * m_head
    count = (length - start).astype(f32)
    pos = first + lax.broadcasted_iota(jnp.int32, (TOK, 1), 0)
    valid = (pos >= start) & (pos < length)
    part = jnp.sum(jnp.where(valid, score, 0.0), axis=0, keepdims=True) / count
    weight = jnp.where(valid, loss_scale / count, 0.0)
    alpha = inv * weight
    beta = inv * inv * weight * score * (1.0 / D)
    up_head = gram[R : R + 1, 128:] + gram[R + 1 : R + 2, 128:]
    back = alpha * up_head - beta * m_up
    pre_grad = back * sig * (1.0 + pre * (1.0 - sig))
    nab = -(act * beta)
    left = jnp.where(unit, pre_grad, pltpu.roll(nab, 32, 1))
    right = jnp.where(lane < 64, nab, pltpu.roll(nab, 64, 1))
    lhs = jnp.concatenate([left, right], axis=1).astype(bf16)
    a_left = jnp.where(unit, 0.0, pltpu.roll(act, 32, 1))
    a_right = jnp.where(lane < 64, act, pltpu.roll(act, 64, 1))
    u_row = jnp.sum(alpha * jnp.concatenate([a_left, a_right], axis=1), axis=0, keepdims=True)
    v_row = jnp.sum(alpha * act, axis=0, keepdims=True)
    low = mm(act_b, lhs, 0, 0)
    low = jnp.where(lanes((128, 256)) < R, 0.0, low)
    row = lax.broadcasted_iota(jnp.int32, (128, 256), 0)
    top = jnp.where((row == R) | (row == R + 1), u_row, 0.0)
    c_hi, c_lo = halves(jnp.concatenate([top, low], axis=0))
    for i in range(D // CH):
        cut = slice(i * CH, (i + 1) * CH)
        w = w_ref[cut, :]
        g_ref[cut, :] = mm(x_ref[:, cut], lhs, 0, 0) + (mm(w, c_hi, 1, 0) + mm(w, c_lo, 1, 0))

    al_hi = alpha.astype(bf16).astype(f32)
    al_lo = alpha - al_hi
    al = jnp.where(lane == 0, al_hi, jnp.where(lane == 1, al_lo, 0.0))
    al = jnp.transpose(al)[:16].astype(bf16)
    v_hi = v_row.astype(bf16).astype(f32)
    row = lax.broadcasted_iota(jnp.int32, (16, 128), 0)
    vv = jnp.where(row == 0, v_hi, jnp.where(row == 1, v_row - v_hi, 0.0)).astype(bf16)
    pooled = mm(al, x_ref[...], 1, 0) + mm(vv, w_ref[:, 128:], 1, 1)
    p_ref[:, D:] = jnp.zeros((8, 256), f32)
    p_ref[:, :D] = jnp.broadcast_to(pooled[0:1] + pooled[1:2], (8, D))

    s_e = level(jnp.abs(part))
    s_v = part * jnp.exp2(s_e * -0.125) * STEPS
    s_hi = jnp.round(s_v)
    s_lo = jnp.round((s_v - s_hi) * FINE)
    one = lanes((1, 128))
    s_row = jnp.where(one == 0, s_e, jnp.where(one == 1, s_hi, jnp.where(one == 2, s_lo, 0.0))).astype(jnp.int32)
    for j in range(NB):
        a = g_ref[j * BW : (j + 1) * BW, :128]
        b0 = g_ref[j * BW : j * BW + BW // 2, 128:]
        b1 = g_ref[j * BW + BW // 2 : (j + 1) * BW, 128:]
        b = jnp.where(lanes((BW // 2, 128)) < 64, b0, b1)
        a_e = level(jnp.max(jnp.abs(a), axis=0, keepdims=True))
        b_e = level(jnp.max(jnp.abs(b), axis=0, keepdims=True))
        out_ref[j, :BW, :] = coded(a, a_e).astype(jnp.int16)
        out_ref[j, BW : BW + BW // 2, :] = coded(b, b_e).astype(jnp.int16)
        base = j * BW // 128 * 128
        window = p_ref[:, base : base + 512]
        off = j * BW - base
        if off:
            window = pltpu.roll(window, 512 - off, 1)
        window = jnp.where(lanes((8, 512)) < BW, window, 0.0)
        p_e = level(jnp.max(jnp.abs(window), axis=1, keepdims=True))
        p_q = coded(window, p_e)
        at = lax.broadcasted_iota(jnp.int32, (16, 128), 0)
        rows = (
            a_e.astype(jnp.int32),
            b_e.astype(jnp.int32),
            p_q[0:1, :128],
            p_q[0:1, 128:256],
            p_q[0:1, 256:384],
            jnp.broadcast_to(p_e[0:1].astype(jnp.int32), (1, 128)),
            s_row,
        )
        meta = jnp.zeros((16, 128), jnp.int32)
        for k, r in enumerate(rows):
            meta = jnp.where(at == k, r, meta)
        out_ref[j, BW + BW // 2 :, :] = meta.astype(jnp.int16)


def block_kernel(info, ranking, q_ref, out_ref):
    mine = info[4]
    place = jnp.int32(0)
    for k in range(16):
        place = jnp.where(ranking[0, k] == mine, jnp.int32(k), place)
    half = BW + BW // 2
    parts = [q_ref[s, half:, :].astype(jnp.int32).astype(f32) for s in range(NB)]
    scale = [jnp.exp2(m * 0.125) for m in parts]
    pooled = [jnp.zeros((1, 128), f32) for _ in range(3)]
    reward = jnp.zeros((1, 128), f32)
    one = lanes((1, 128))
    for s in range(NB):
        m, e = parts[s], scale[s] * (1.0 / STEPS)
        for k in range(3):
            pooled[k] = pooled[k] + m[2 + k : 3 + k] * e[5:6]
        told = jnp.where(one == 1, m[6:7], jnp.where(one == 2, m[6:7] * (1.0 / FINE), 0.0))
        told = jnp.sum(told, axis=1, keepdims=True)
        by = jnp.sum(jnp.where(one == 0, e[6:7], 0.0), axis=1, keepdims=True)
        reward = reward + told * by
    at = lax.broadcasted_iota(jnp.int32, (16, 128), 0)
    tail = jnp.zeros((16, 128), f32)
    for k in range(3):
        tail = jnp.where(at == k, pooled[k], tail)
    meta = jnp.where(one < 64, reward, place.astype(f32))
    meta = jnp.broadcast_to(meta, (8, 128))
    for i in range(32):
        if i < half // 16:
            which = 0 if i < BW // 16 else 1
            acc = jnp.zeros((16, 128), f32)
            for s in range(NB):
                v = q_ref[s, i * 16 : (i + 1) * 16, :].astype(jnp.int32).astype(f32)
                acc = acc + v * (scale[s][which : which + 1] * (1.0 / STEPS))
        elif i == half // 16:
            acc = tail
        else:
            acc = jnp.zeros((16, 128), f32)
        out_ref[i, :16, :] = acc
        out_ref[i, 16:, :] = meta


def slope_kernel(info, d_ref, out_ref, loss_ref):
    told = d_ref[:, 16, :]
    lane = lanes((32, 128))
    row = lax.broadcasted_iota(jnp.int32, (32, 128), 0)
    r_col = jnp.sum(jnp.where(lane == 0, told, 0.0), axis=1, keepdims=True)
    k_col = jnp.sum(jnp.where(lane == 64, told, 0.0), axis=1, keepdims=True)
    r_row = jnp.sum(jnp.where(lane == row, r_col, 0.0), axis=0, keepdims=True)
    k_row = jnp.sum(jnp.where(lane == row, k_col, 0.0), axis=0, keepdims=True)
    real = lane < 32
    later = real & ((lane & 1) == (row & 1)) & (k_col >= k_row)
    top = jnp.max(jnp.where(later, r_col, -1e30), axis=0, keepdims=True)
    top = jnp.where(real[0:1], top, 0.0)
    ex = jnp.where(later, jnp.exp(jnp.where(later, r_col - top, 0.0)), 0.0)
    total = jnp.where(real[0:1], jnp.sum(ex, axis=0, keepdims=True), 1.0)
    slope = jnp.sum(ex / total, axis=1, keepdims=True) - 1.0
    terms = top + jnp.log(total) - r_row
    terms = jnp.where(real[0:1] & ((lane[0:1] & 1) == info[5]), terms, 0.0)
    loss_ref[...] = jnp.broadcast_to(jnp.sum(terms, axis=1, keepdims=True), (8, 128))
    acc = jnp.zeros((16, 128), f32)
    for i in range(32):
        acc = acc + d_ref[i, :16, :] * slope[i : i + 1]
    for i in range(32):
        out_ref[i] = acc


def on_device(hidden, lengths, starts, ranking, down_w, up_w, gain, head):
    x = hidden[0, 0]
    cand, fsdp, prompt = lax.axis_index("cand"), lax.axis_index("fsdp"), lax.axis_index("prompt")
    core = cand % 2
    gain_f, head_f = gain.astype(f32), head.astype(f32)
    both = gain_f * head_f
    near = lax.reduce_precision(both, 8, 7)
    hg_hi, hg_lo = near.astype(bf16), (both - near).astype(bf16)
    pad = jnp.zeros((BW, 128 - R), bf16)
    down_t = jnp.concatenate([down_w.T, hg_hi[:, None], hg_lo[:, None], pad[:, 2:]], axis=1)
    up_t = jnp.concatenate([up_w.T, pad], axis=1)
    slab = jnp.where(core == 0, down_t, up_t)
    mine = lax.all_to_all(jnp.broadcast_to(slab[None], (NB, BW, 128)), "fsdp", 0, 0, tiled=True)
    mine = mine.reshape(D, 128)
    other = lax.ppermute(mine, "cand", [(i, i ^ 1) for i in range(16)])
    info = jnp.stack([starts[0, 0], lengths[0, 0], fsdp * TOK, core, cand, prompt]).astype(jnp.int32)
    rows = BW + BW // 2 + 16
    coded_terms = pl.pallas_call(
        local_kernel,
        out_shape=jax.ShapeDtypeStruct((NB, rows, 128), jnp.int16),
        in_specs=[SMEM, VMEM, VMEM, VMEM],
        out_specs=VMEM,
        scratch_shapes=[
            pltpu.VMEM((D, 256), bf16),
            pltpu.VMEM((TOK, 1), f32),
            pltpu.VMEM((D, 256), f32),
            pltpu.VMEM((8, D + 256), f32),
        ],
        compiler_params=pltpu.CompilerParams(vmem_limit_bytes=48 << 20),
    )(info, x, mine, other)
    swapped = lax.all_to_all(coded_terms, "fsdp", 0, 0, tiled=True)
    sums = pl.pallas_call(
        block_kernel,
        out_shape=jax.ShapeDtypeStruct((32, 24, 128), f32),
        in_specs=[SMEM, SMEM, VMEM],
        out_specs=VMEM,
        compiler_params=pltpu.CompilerParams(vmem_limit_bytes=16 << 20),
    )(info, ranking, swapped)
    pieces = lax.all_to_all(sums, ("cand", "prompt"), 0, 0, tiled=True)
    share, loss = pl.pallas_call(
        slope_kernel,
        out_shape=(jax.ShapeDtypeStruct((32, 16, 128), f32), jax.ShapeDtypeStruct((8, 128), f32)),
        in_specs=[SMEM, VMEM],
        out_specs=(VMEM, VMEM),
        compiler_params=pltpu.CompilerParams(vmem_limit_bytes=16 << 20),
    )(info, pieces)
    final = lax.all_to_all(share, ("cand", "prompt"), 0, 0, tiled=True).reshape(512, 128)
    half = BW + BW // 2
    slab_a, slab_b = final[:BW], final[BW:half]
    pooled = final[half : half + 3].reshape(-1)[:BW]
    down_grad = slab_a[:, :R].T
    up_low = jnp.concatenate([slab_b[:, :64], slab_b[:, 64:]], axis=0)
    up_grad = jnp.concatenate([up_low, slab_a[:, R:]], axis=1).T
    return (loss[0, :1], down_grad, up_grad, head_f * pooled, gain_f * pooled)


def solution(mesh):
    placed = (
        P("prompt", "cand", "fsdp", None),
        P("prompt", "cand"),
        P("prompt", "cand"),
        P("prompt", None),
        P(None, "fsdp"),
        P(None, "fsdp"),
        P("fsdp"),
        P("fsdp"),
    )
    return jax.shard_map(
        on_device,
        mesh=mesh,
        in_specs=placed,
        out_specs=(P("prompt"), P(None, "fsdp"), P(None, "fsdp"), P("fsdp"), P("fsdp")),
        check_vma=False,
    )
```

time: 946 us -> 161 us (0.17)
  waiting for transfers between devices: 500 us -> 12 us
  blocking collectives: 366 us -> 113 us
  matrix products: 28.2 us -> 0 us
  Pallas kernels: 0 us -> 17.6 us
  between operations: 17.9 us -> 2.05 us
  local copies, waits for them, and re-layouts: 17 us -> 2.22 us
  other arithmetic: 15.4 us -> 3.07 us
  starting transfers between devices: 0.3 us -> 10.6 us
    unnamed x5 -> x0, waiting for transfers between devices: 407 us -> none
    unnamed x3 -> x0, blocking collectives: 184 us -> none
    all_to_all x0 -> x3, blocking collectives: none -> 113 us  [the longest x1 46.8 us: on_device(): swapped = lax.all_to_all(coded_terms, 'fsdp', 0, 0, tiled=True)]
    psum x2 -> x0, blocking collectives: 102 us -> none  [the longest x1 71.4 us: on_device(): lax.psum((terms[0], terms[1], terms[2], terms[3]), ('cand', 'prompt'))]
    psum x1 -> x0, waiting for transfers between devices: 93.8 us -> none  [on_device(): lax.psum((terms[0], terms[1], terms[2], terms[3]), ('cand', 'prompt'))]
    all_gather x2 -> x0, blocking collectives: 80.1 us -> none  [the longest x1 43 us: on_device(): lax.all_gather(down_w, 'fsdp', axis=1, tiled=True)]
    pallas_call x0 -> x3, Pallas kernels: none -> 17.6 us  [the longest x1 15 us: on_device(): pl.pallas_call(local_kernel, out_shape=jax.ShapeDtypeStruct((NB, rows, 12...]
    dot_general x3 -> x0, matrix products: 16.6 us -> none  [the longest x1 7.46 us: token_backward(): pooled = jnp.dot(weight, scaled, precision=lax.Precision.HIGHEST)]
  transfers between devices with their start and end apart: 3 -> 2, of which waited for: 3 -> 2; matrix products, arithmetic and copies ran while one was open for 2% -> 0% of each run, Pallas kernels for 0% -> 0%
where the time goes in v1:
time: 161 us; the launch traced here: 160 us
  blocking collectives  113 us (70%)
  Pallas kernels  17.6 us (11%)
  waiting for transfers between devices  12 us (7%)
  starting transfers between devices  10.6 us (7%)
  other arithmetic  3.07 us (2%)
  local copies, waits for them, and re-layouts  2.22 us (1%)
  between operations  2.05 us (1%)
    all_to_all x1, blocking collectives, on_device(): swapped = lax.all_to_all(coded_terms, 'fsdp', 0, 0, tiled=True)  46.8 us
    all_to_all x1, blocking collectives, on_device(): lax.all_to_all(jnp.broadcast_to(slab[None], (NB, BW, 128)), 'fsdp', 0, 0,...  40 us
    all_to_all x1, blocking collectives, on_device(): pieces = lax.all_to_all(sums, ('cand', 'prompt'), 0, 0, tiled=True)  26 us
    pallas_call x1, Pallas kernels, on_device(): pl.pallas_call(local_kernel, out_shape=jax.ShapeDtypeStruct((NB, rows, 12...  15 us
    all_to_all x1, waiting for transfers between devices, on_device(): lax.all_to_all(share, ('cand', 'prompt'), 0, 0, tiled=True)  11 us
    ppermute x1, starting transfers between devices, on_device(): other = lax.ppermute(mine, 'cand', [(i, i ^ 1) for i in range(16)])  5.45 us
    all_to_all x1, starting transfers between devices, on_device(): lax.all_to_all(share, ('cand', 'prompt'), 0, 0, tiled=True)  5.15 us
  transfers between devices with their start and end apart: 2, of which 2 were waited for; matrix products, arithmetic and copies ran while one was open for 0% of the time, Pallas kernels for 0%

profile of v1, /device:TPU:1, one launch (start us, length us, event | category | flops | bytes accessed | tf_op | source)
XLA Modules:
  0.0 160.4 jit_solution(17172262844966562669)
XLA Ops:
  0.6 0.7 reduce-precision_convert_fusion
  1.4 0.1 pad.7.clone
  1.4 1.0 maximum_select_fusion
  2.5 0.1 copy.13
  2.6 0.2 broadcast_in_dim.15
  2.8 40.0 %all_to_all.20 = bf16[16,288,128]{2,1,0:T(8,128)(2,1)S(1)} all-to-all(bf16[16,288,128]{2,1,0:T(8,128)(2,1)S(1)} %broadcast_in_dim.15), channel_id=1, replica_groups=mesh['cand'=16,'fsdp'=16,'prompt'=2] {'fsdp'}, dimensions={0} | all-to-all | bytes 2359296 | tf_op jit(solution)/shard_map/all_to_all | solution.py:239
  42.7 5.5 %collective-permute-start = (bf16[4608,128]{1,0:T(8,128)(2,1)S(1)}, bf16[4608,128]{1,0:T(8,128)(2,1)S(1)}, u32[]{:S(2)}, u32[]{:S(2)}) collective-permute-start(bf16[4608,128]{1,0:T(8,128)(2,1)S(1)} %bitcast.22), channel_id=1, source_target_pairs={{0,32},{32,0},{64,96},{96,64},{128,160},{160,128},{192,224},{224,1... | collective-permute-start | bytes 3538952 | tf_op jit(solution)/shard_map/ppermute | solution.py:241
  49.5 0.1 stack.19.info
  49.6 1.1 collective-permute-done.other_ref
  50.6 15.0 %shard_map.119 = s16[16,448,128]{2,1,0:T(8,128)(2,1)S(1)} custom-call(s32[6]{0:T(128)S(1)} %stack.19.info, bf16[512,4608]{1,0:T(8,128)(2,1)} %bitcast.24, bf16[4608,128]{1,0:T(8,128)(2,1)S(1)} %bitcast.23, bf16[4608,128]{1,0:T(8,128)(2,1)S(1)} %collective-permute-done.other_ref), custom_call_target="tpu_custom_call" | custom-call | tf_op jit(solution)/shard_map/pallas_call | solution.py:244
  65.7 0.0 copy-start
  65.7 46.8 %all_to_all.21.q_ref = s16[16,448,128]{2,1,0:T(8,128)(2,1)S(1)} all-to-all(s16[16,448,128]{2,1,0:T(8,128)(2,1)S(1)} %shard_map.119), channel_id=1, replica_groups=mesh['cand'=16,'fsdp'=16,'prompt'=2] {'fsdp'}, dimensions={0} | all-to-all | bytes 3670016 | tf_op jit(solution)/shard_map/all_to_all | solution.py:257
  112.5 0.0 copy-done
  112.5 0.0 copy-start.1
  112.5 0.0 copy-start.2
  112.5 1.1 shard_map.120
  113.6 26.0 %all_to_all.22.d_ref = f32[32,24,128]{2,1,0:T(8,128)S(1)} all-to-all(f32[32,24,128]{2,1,0:T(8,128)S(1)} %shard_map.120), channel_id=1, replica_groups=mesh['cand'=16,'fsdp'=16,'prompt'=2] {'cand','prompt'}, dimensions={0} | all-to-all | bytes 786432 | tf_op jit(solution)/shard_map/all_to_all | solution.py:265
  139.6 1.5 shard_map.121
  141.1 5.2 %all-to-all-start.3 = ((f32[32,16,128]{2,1,0:T(8,128)}), f32[32,16,128]{2,1,0:T(8,128)S(1)}, u32[]{:S(2)}, u32[]{:S(2)}) async-start(f32[32,16,128]{2,1,0:T(8,128)} %get-tuple-element.8), calls=%async_computation.3 | async-start | bytes 524288 | tf_op jit(solution)/shard_map/all_to_all | solution.py:273
  146.3 0.5 slice.37
  146.8 11.0 %all-to-all-done.3 = f32[32,16,128]{2,1,0:T(8,128)S(1)} async-done(((f32[32,16,128]{2,1,0:T(8,128)}), f32[32,16,128]{2,1,0:T(8,128)S(1)}, u32[]{:S(2)}, u32[]{:S(2)}) %all-to-all-start.3) | async-done | bytes 262176 | tf_op jit(solution)/shard_map/all_to_all | solution.py:273
  157.7 0.0 copy-done.1
  157.7 0.0 copy-done.2
  157.7 0.6 convert_multiply_fusion.2
  158.3 0.1 fusion.1
  158.4 0.1 copy.19
  158.5 0.1 copy.20
  158.6 0.1 slice.53
  158.7 0.8 copy.18
  159.5 0.1 copy.21
  159.6 0.8 maximum_bitcast_fusion
  (6 shorter events, 0.0 us)
Async XLA Ops:
  42.7 7.9 %collective-permute-start = (bf16[4608,128]{1,0:T(8,128)(2,1)S(1)}, bf16[4608,128]{1,0:T(8,128)(2,1)S(1)}, u32[]{:S(2)}, u32[]{:S(2)}) collective-permute-start(bf16[4608,128]{1,0:T(8,128)(2,1)S(1)} %bitcast.22), channel_id=1, source_target_pairs={{0,32},{32,0},{64,96},{96,64},{128,160},{160,128},{192,224},{224,1... | collective-permute-start | bytes 3538952 | tf_op jit(solution)/shard_map/ppermute | solution.py:241
  65.7 46.8 %copy-start = (s32[1,16]{1,0:T(1,128)S(1)}, s32[1,16]{1,0:T(1,128)}, u32[]{:S(2)}) copy-start(s32[1,16]{1,0:T(1,128)} %ranking.1) | copy-start | bytes 196
  112.5 45.2 %copy-start.1 = (bf16[288]{0:T(512)(128)(2,1)S(1)}, bf16[288]{0:T(512)(128)(2,1)}, u32[]{:S(2)}) copy-start(bf16[288]{0:T(512)(128)(2,1)} %param.15) | copy-start | bytes 1732
  112.5 45.2 %copy-start.2 = (bf16[288]{0:T(512)(128)(2,1)S(1)}, bf16[288]{0:T(512)(128)(2,1)}, u32[]{:S(2)}) copy-start(bf16[288]{0:T(512)(128)(2,1)} %param.14) | copy-start | bytes 1732
  141.1 16.6 %all-to-all-start.3 = ((f32[32,16,128]{2,1,0:T(8,128)}), f32[32,16,128]{2,1,0:T(8,128)S(1)}, u32[]{:S(2)}, u32[]{:S(2)}) async-start(f32[32,16,128]{2,1,0:T(8,128)} %get-tuple-element.8), calls=%async_computation.3 | async-start | bytes 524288 | tf_op jit(solution)/shard_map/all_to_all | solution.py:273

commit v2 on v1

--- a/solution.py
+++ b/solution.py
@@ -1,5 +1,3 @@
-import functools
-
 import jax
 import jax.numpy as jnp
 from jax import lax
@@ -13,6 +11,7 @@
 TOK = 512
 NB = 16
 BW = 288
+HALF = 2304
 CH = 512
 STEPS = 32760.0
 FINE = 60000.0
@@ -44,28 +43,90 @@
     return jnp.round(v * jnp.exp2(e * -0.125) * STEPS).astype(jnp.int32)
 
 
-def local_kernel(info, x_ref, mine_ref, other_ref, out_ref, w_ref, ss_ref, g_ref, p_ref):
-    start, length, first, core = info[0], info[1], info[2], info[3]
-
-    @pl.when(core == 0)
-    def _():
-        w_ref[:, :128] = mine_ref[...]
-        w_ref[:, 128:] = other_ref[...]
-
-    @pl.when(core != 0)
-    def _():
-        w_ref[:, :128] = other_ref[...]
-        w_ref[:, 128:] = mine_ref[...]
+def pack_kernel(w_ref, out_ref):
+    w = w_ref[...].astype(f32)
+    w = jnp.concatenate([w, jnp.zeros((128, 96), f32)], axis=1)
+    t = jnp.transpose(w)
+    lane = lanes((64, 128))
+    last = t[224:288]
+    for i in range(3):
+        cut = slice(64 * i, 64 * i + 64)
+        rows = jnp.where(lane < R, t[cut], pltpu.roll(last, 96 - 32 * i, 1)).astype(bf16)
+        for j in range(8):
+            out_ref[j, cut, :] = rows
+    lane = lanes((32, 128))
+    rows = jnp.where(lane < R, t[192:224], 0.0)
+    for k in range(9):
+        piece = t[32 * k : 32 * k + 32]
+        rows = jnp.where(lane == R + k, pltpu.roll(piece, k, 1) if k else piece, rows)
+    rows = rows.astype(bf16)
+    for j in range(8):
+        out_ref[j, 192:, :] = rows
+
+
+def unpack(q_ref, store):
+    for j in range(8):
+        q = q_ref[j].astype(f32)
+        lane = lanes((32, 128))
+        part = q[192:]
+        cols = [pltpu.roll(part, 128 - k, 1) if k else part for k in range(9)]
+        for k in range(7):
+            rows = jnp.where(lane < R, q[32 * k : 32 * k + 32], jnp.where(lane == R, cols[k], 0.0))
+            store(j * BW + 32 * k, rows.astype(bf16))
+        for k in range(2):
+            cut = [pltpu.roll(q[64 * i + 32 * k : 64 * i + 32 * k + 32], 32 * i + 32, 1) for i in range(3)]
+            rows = jnp.where(lane < 32, cut[0], jnp.where(lane < 64, cut[1], cut[2]))
+            rows = jnp.where(lane < R, rows, jnp.where(lane == R, cols[7 + k], 0.0))
+            store(j * BW + 224 + 32 * k, rows.astype(bf16))
+
+
+def unpack_both(core, mine_ref, other_ref, w_ref):
+    def stores(left):
+        def to_left(at, rows):
+            w_ref[at : at + 32, :128] = rows
+
+        def to_right(at, rows):
+            w_ref[at : at + 32, 128:] = rows
+
+        return (to_left, to_right) if left else (to_right, to_left)
+
+    for left in (True, False):
+
+        @pl.when((core == 0) == left)
+        def _(left=left):
+            first, second = stores(left)
+            unpack(mine_ref, first)
+            unpack(other_ref, second)
+
+
+def near_kernel(x_ref, mine_ref, other_ref, w_ref, prod_ref, gram_ref, ss_ref):
+    unpack_both(lax.axis_index("cand") % 2, mine_ref, other_ref, w_ref)
 
     def square(i, carry):
-        rows = x_ref[pl.ds(pl.multiple_of(i * 16, 16), 16), :].astype(f32)
-        ss_ref[pl.ds(pl.multiple_of(i * 16, 16), 16), :] = jnp.sum(rows * rows, axis=1, keepdims=True)
+        at = pl.ds(pl.multiple_of(i * 16, 16), 16)
+        rows = x_ref[at, :].astype(f32)
+        ss_ref[at, :] = jnp.broadcast_to(jnp.sum(rows * rows, axis=1, keepdims=True), (16, 128))
         return carry
 
     lax.fori_loop(0, TOK // 16, square, 0)
-
-    prod = mm(x_ref[...], w_ref[...], 1, 0)
-    gram = mm(w_ref[...], w_ref[...], 0, 0)
+    cols = pl.ds(pl.multiple_of(lax.axis_index("fsdp") // 8 * HALF, 128), HALF)
+    prod_ref[...] = mm(x_ref[:, cols], w_ref[...], 1, 0)
+    gram_ref[...] = mm(w_ref[...], w_ref[...], 0, 0)
+
+
+def local_kernel(
+    starts, lengths, x_ref, w_near, prod_near, gram_near, ss_ref, mine_ref, other_ref, out_ref, w_far, w_ref, g_ref, p_ref
+):
+    start, length = starts[0, 0], lengths[0, 0]
+    first = lax.axis_index("fsdp") * TOK
+    core = lax.axis_index("cand") % 2
+    side = lax.axis_index("fsdp") // 8
+    unpack_both(core, mine_ref, other_ref, w_far)
+    w_ref[pl.ds(pl.multiple_of(side * HALF, 256), HALF), :] = w_near[...]
+    w_ref[pl.ds(pl.multiple_of((1 - side) * HALF, 256), HALF), :] = w_far[...]
+    cols = pl.ds(pl.multiple_of((1 - side) * HALF, 128), HALF)
+    prod = prod_near[...] + mm(x_ref[:, cols], w_far[...], 1, 0)
+    gram = gram_near[...] + mm(w_far[...], w_far[...], 0, 0)
     pre = prod[:, :128]
     x_up = prod[:, 128:]
     lane = lanes((TOK, 128))
@@ -77,8 +138,8 @@
     through = mm(act_b, g_hi, 1, 0) + mm(act_b, g_lo, 1, 0)
     m_left = pre + through[:, :128]
     m_up = x_up + through[:, 128:]
-    m_head = jnp.sum(jnp.where((lane == R) | (lane == R + 1), m_left, 0.0), axis=1, keepdims=True)
-    m_sq = ss_ref[...] + jnp.sum(act * (x_up + m_up), axis=1, keepdims=True)
+    m_head = jnp.sum(jnp.where(lane == R, m_left + m_up, 0.0), axis=1, keepdims=True)
+    m_sq = ss_ref[:, :1] + jnp.sum(act * (x_up + m_up), axis=1, keepdims=True)
     inv = lax.rsqrt(jnp.maximum(m_sq, 0.0) * (1.0 / D) + 1e-06)
     score = inv * m_head
     count = (length - start).astype(f32)
@@ -88,7 +149,7 @@
     weight = jnp.where(valid, loss_scale / count, 0.0)
     alpha = inv * weight
     beta = inv * inv * weight * score * (1.0 / D)
-    up_head = gram[R : R + 1, 128:] + gram[R + 1 : R + 2, 128:]
+    up_head = gram[R : R + 1, 128:] + gram[128 + R : 129 + R, 128:]
     back = alpha * up_head - beta * m_up
     pre_grad = back * sig * (1.0 + pre * (1.0 - sig))
     nab = -(act * beta)
@@ -102,7 +163,8 @@
     low = mm(act_b, lhs, 0, 0)
     low = jnp.where(lanes((128, 256)) < R, 0.0, low)
     row = lax.broadcasted_iota(jnp.int32, (128, 256), 0)
-    top = jnp.where((row == R) | (row == R + 1), u_row, 0.0)
+    top = jnp.where(row == R, u_row, 0.0)
+    low = jnp.where(row == R, u_row, low)
     c_hi, c_lo = halves(jnp.concatenate([top, low], axis=0))
     for i in range(D // CH):
         cut = slice(i * CH, (i + 1) * CH)
@@ -159,8 +221,8 @@
         out_ref[j, BW + BW // 2 :, :] = meta.astype(jnp.int16)
 
 
-def block_kernel(info, ranking, q_ref, out_ref):
-    mine = info[4]
+def block_kernel(ranking, q_ref, out_ref):
+    mine = lax.axis_index("cand")
     place = jnp.int32(0)
     for k in range(16):
         place = jnp.where(ranking[0, k] == mine, jnp.int32(k), place)
@@ -184,99 +246,122 @@
         tail = jnp.where(at == k, pooled[k], tail)
     meta = jnp.where(one < 64, reward, place.astype(f32))
     meta = jnp.broadcast_to(meta, (8, 128))
-    for i in range(32):
+    for i in range(28):
         if i < half // 16:
             which = 0 if i < BW // 16 else 1
             acc = jnp.zeros((16, 128), f32)
             for s in range(NB):
                 v = q_ref[s, i * 16 : (i + 1) * 16, :].astype(jnp.int32).astype(f32)
                 acc = acc + v * (scale[s][which : which + 1] * (1.0 / STEPS))
-        elif i == half // 16:
+        else:
             acc = tail
-        else:
-            acc = jnp.zeros((16, 128), f32)
-        out_ref[i, :16, :] = acc
-        out_ref[i, 16:, :] = meta
-
-
-def slope_kernel(info, d_ref, out_ref, loss_ref):
-    told = d_ref[:, 16, :]
-    lane = lanes((32, 128))
-    row = lax.broadcasted_iota(jnp.int32, (32, 128), 0)
+        for g in (2 * i, 2 * i + 1):
+            at = g % 7 * 8
+            out_ref[g // 7, at : at + 8, :] = acc[g % 2 * 8 : g % 2 * 8 + 8]
+    for i in range(8):
+        out_ref[i, 56:, :] = meta
+
+
+def slope_kernel(d_ref, o_ref, out_ref, loss_ref):
+    told = jnp.concatenate([d_ref[:, 56, :], o_ref[:, 56, :]], axis=0)
+    lane = lanes((16, 128))
+    row = lax.broadcasted_iota(jnp.int32, (16, 128), 0)
     r_col = jnp.sum(jnp.where(lane == 0, told, 0.0), axis=1, keepdims=True)
     k_col = jnp.sum(jnp.where(lane == 64, told, 0.0), axis=1, keepdims=True)
     r_row = jnp.sum(jnp.where(lane == row, r_col, 0.0), axis=0, keepdims=True)
     k_row = jnp.sum(jnp.where(lane == row, k_col, 0.0), axis=0, keepdims=True)
-    real = lane < 32
-    later = real & ((lane & 1) == (row & 1)) & (k_col >= k_row)
+    real = lane < 16
+    later = real & (k_col >= k_row)
     top = jnp.max(jnp.where(later, r_col, -1e30), axis=0, keepdims=True)
     top = jnp.where(real[0:1], top, 0.0)
     ex = jnp.where(later, jnp.exp(jnp.where(later, r_col - top, 0.0)), 0.0)
     total = jnp.where(real[0:1], jnp.sum(ex, axis=0, keepdims=True), 1.0)
     slope = jnp.sum(ex / total, axis=1, keepdims=True) - 1.0
-    terms = top + jnp.log(total) - r_row
-    terms = jnp.where(real[0:1] & ((lane[0:1] & 1) == info[5]), terms, 0.0)
+    terms = jnp.where(real[0:1], top + jnp.log(total) - r_row, 0.0)
     loss_ref[...] = jnp.broadcast_to(jnp.sum(terms, axis=1, keepdims=True), (8, 128))
-    acc = jnp.zeros((16, 128), f32)
-    for i in range(32):
-        acc = acc + d_ref[i, :16, :] * slope[i : i + 1]
-    for i in range(32):
-        out_ref[i] = acc
+    acc = jnp.zeros((56, 128), f32)
+    for i in range(8):
+        acc = acc + d_ref[i, :56, :] * slope[i : i + 1] + o_ref[i, :56, :] * slope[8 + i : 9 + i]
+    out_ref[...] = acc
 
 
 def on_device(hidden, lengths, starts, ranking, down_w, up_w, gain, head):
     x = hidden[0, 0]
-    cand, fsdp, prompt = lax.axis_index("cand"), lax.axis_index("fsdp"), lax.axis_index("prompt")
-    core = cand % 2
-    gain_f, head_f = gain.astype(f32), head.astype(f32)
-    both = gain_f * head_f
+    core = lax.axis_index("cand") % 2
+    sibling = [(i, i ^ 1) for i in range(16)]
+    both = gain.astype(f32) * head.astype(f32)
     near = lax.reduce_precision(both, 8, 7)
-    hg_hi, hg_lo = near.astype(bf16), (both - near).astype(bf16)
-    pad = jnp.zeros((BW, 128 - R), bf16)
-    down_t = jnp.concatenate([down_w.T, hg_hi[:, None], hg_lo[:, None], pad[:, 2:]], axis=1)
-    up_t = jnp.concatenate([up_w.T, pad], axis=1)
-    slab = jnp.where(core == 0, down_t, up_t)
-    mine = lax.all_to_all(jnp.broadcast_to(slab[None], (NB, BW, 128)), "fsdp", 0, 0, tiled=True)
-    mine = mine.reshape(D, 128)
-    other = lax.ppermute(mine, "cand", [(i, i ^ 1) for i in range(16)])
-    info = jnp.stack([starts[0, 0], lengths[0, 0], fsdp * TOK, core, cand, prompt]).astype(jnp.int32)
+    part = jnp.where(core == 0, near, both - near).astype(bf16)
+    half_w = jnp.where(core == 0, down_w, up_w)
+    half_w = jnp.concatenate([half_w, jnp.broadcast_to(part[None], (32, BW))], axis=0)
+    packed = pl.pallas_call(
+        pack_kernel,
+        out_shape=jax.ShapeDtypeStruct((8, 224, 128), bf16),
+        in_specs=[VMEM],
+        out_specs=VMEM,
+        compiler_params=pltpu.CompilerParams(vmem_limit_bytes=16 << 20),
+    )(half_w)
+    along_y = [list(range(8)), list(range(8, 16))]
+    mine = lax.all_to_all(packed, "fsdp", 0, 0, axis_index_groups=along_y, tiled=True)
+    across = [(i, i ^ 8) for i in range(16)]
+    far_mine = lax.ppermute(mine, "fsdp", across)
+    other = lax.ppermute(mine, "cand", sibling)
+    w_near, prod, gram, squares = pl.pallas_call(
+        near_kernel,
+        out_shape=(
+            jax.ShapeDtypeStruct((HALF, 256), bf16),
+            jax.ShapeDtypeStruct((TOK, 256), f32),
+            jax.ShapeDtypeStruct((256, 256), f32),
+            jax.ShapeDtypeStruct((TOK, 128), f32),
+        ),
+        in_specs=[VMEM, VMEM, VMEM],
+        out_specs=(VMEM, VMEM, VMEM, VMEM),
+        compiler_params=pltpu.CompilerParams(vmem_limit_bytes=24 << 20),
+    )(x, mine, other)
+    far_mine, squares = lax.optimization_barrier((far_mine, squares))
+    far_other = lax.ppermute(far_mine, "cand", sibling)
     rows = BW + BW // 2 + 16
     coded_terms = pl.pallas_call(
         local_kernel,
         out_shape=jax.ShapeDtypeStruct((NB, rows, 128), jnp.int16),
-        in_specs=[SMEM, VMEM, VMEM, VMEM],
+        in_specs=[SMEM, SMEM] + [VMEM] * 7,
         out_specs=VMEM,
         scratch_shapes=[
+            pltpu.VMEM((HALF, 256), bf16),
             pltpu.VMEM((D, 256), bf16),
-            pltpu.VMEM((TOK, 1), f32),
             pltpu.VMEM((D, 256), f32),
             pltpu.VMEM((8, D + 256), f32),
         ],
-        compiler_params=pltpu.CompilerParams(vmem_limit_bytes=48 << 20),
-    )(info, x, mine, other)
+        compiler_params=pltpu.CompilerParams(vmem_limit_bytes=40 << 20),
+    )(starts, lengths, x, w_near, prod, gram, squares, far_mine, far_other)
     swapped = lax.all_to_all(coded_terms, "fsdp", 0, 0, tiled=True)
     sums = pl.pallas_call(
         block_kernel,
-        out_shape=jax.ShapeDtypeStruct((32, 24, 128), f32),
-        in_specs=[SMEM, SMEM, VMEM],
+        out_shape=jax.ShapeDtypeStruct((8, 64, 128), f32),
+        in_specs=[SMEM, VMEM],
         out_specs=VMEM,
         compiler_params=pltpu.CompilerParams(vmem_limit_bytes=16 << 20),
-    )(info, ranking, swapped)
-    pieces = lax.all_to_all(sums, ("cand", "prompt"), 0, 0, tiled=True)
+    )(ranking, swapped)
+    along_z = [list(range(0, 16, 2)), list(range(1, 16, 2))]
+    pieces = lax.all_to_all(sums, "cand", 0, 0, axis_index_groups=along_z, tiled=True)
+    beside = lax.ppermute(pieces, "cand", sibling)
     share, loss = pl.pallas_call(
         slope_kernel,
-        out_shape=(jax.ShapeDtypeStruct((32, 16, 128), f32), jax.ShapeDtypeStruct((8, 128), f32)),
-        in_specs=[SMEM, VMEM],
+        out_shape=(jax.ShapeDtypeStruct((56, 128), f32), jax.ShapeDtypeStruct((8, 128), f32)),
+        in_specs=[VMEM, VMEM],
         out_specs=(VMEM, VMEM),
         compiler_params=pltpu.CompilerParams(vmem_limit_bytes=16 << 20),
-    )(info, pieces)
-    final = lax.all_to_all(share, ("cand", "prompt"), 0, 0, tiled=True).reshape(512, 128)
+    )(pieces, beside)
+    share = share + lax.ppermute(share, "prompt", [(0, 1), (1, 0)])
+    final = jnp.broadcast_to(share[None], (8, 56, 128))
+    final = lax.all_to_all(final, "cand", 0, 0, axis_index_groups=along_z, tiled=True).reshape(448, 128)
     half = BW + BW // 2
     slab_a, slab_b = final[:BW], final[BW:half]
     pooled = final[half : half + 3].reshape(-1)[:BW]
     down_grad = slab_a[:, :R].T
     up_low = jnp.concatenate([slab_b[:, :64], slab_b[:, 64:]], axis=0)
     up_grad = jnp.concatenate([up_low, slab_a[:, R:]], axis=1).T
+    gain_f, head_f = gain.astype(f32), head.astype(f32)
     return (loss[0, :1], down_grad, up_grad, head_f * pooled, gain_f * pooled)
 
 

time: 161 us -> 154 us (0.957); the launches traced: 160 us -> 151 us
  blocking collectives: 113 us -> 88.6 us
  starting transfers between devices: 10.6 us -> 23.4 us
  Pallas kernels: 17.6 us -> 13.8 us
  waiting for transfers between devices: 12 us -> 15.3 us
  local copies, waits for them, and re-layouts: 2.22 us -> 5.33 us
    all_to_all x2, blocking collectives: 66 us -> 40.6 us  [the longest x1 21.3 us: on_device(): lax.all_to_all(packed, 'fsdp', 0, 0, axis_index_groups=along_y, tiled=True)]
    ppermute x1 -> x5, starting transfers between devices: 5.45 us -> 20 us  [the longest x1 5.24 us: on_device(): beside = lax.ppermute(pieces, 'cand', sibling)]
    pallas_call x1, Pallas kernels: 15 us -> 6.93 us  [on_device(): pl.pallas_call(local_kernel, out_shape=jax.ShapeDtypeStruct((NB, rows, 12...]
    ppermute x1 -> x5, waiting for transfers between devices: 1.07 us -> 6.75 us  [the longest x1 3.1 us: on_device(): far_mine = lax.ppermute(mine, 'fsdp', across)]
    pallas_call x2 -> x4, Pallas kernels: 2.56 us -> 6.89 us  [the longest x1 5.42 us: on_device(): pl.pallas_call(near_kernel, out_shape=(jax.ShapeDtypeStruct((HALF, 256),...]
    unnamed x10 -> x12, local copies, waits for them, and re-layouts: 1.06 us -> 3.93 us
    all_to_all x1, waiting for transfers between devices: 11 us -> 8.57 us  [on_device(): lax.all_to_all(final, 'cand', 0, 0, axis_index_groups=along_z, tiled=True)]
    all_to_all x1, starting transfers between devices: 5.15 us -> 3.4 us  [on_device(): lax.all_to_all(final, 'cand', 0, 0, axis_index_groups=along_z, tiled=True)]
  transfers between devices with their start and end apart: 2 -> 6, of which waited for: 2 -> 5; matrix products, arithmetic and copies ran while one was open for 0% -> 0% of each run, Pallas kernels for 0% -> 4%
where the time goes in v2:
time: 154 us; the launch traced here: 151 us
  blocking collectives  88.6 us (58%)
  starting transfers between devices  23.4 us (15%)
  waiting for transfers between devices  15.3 us (10%)
  Pallas kernels  13.8 us (9%)
  local copies, waits for them, and re-layouts  5.33 us (3%)
  other arithmetic  2.32 us (2%)
  between operations  2.13 us (1%)
    all_to_all x1, blocking collectives, on_device(): swapped = lax.all_to_all(coded_terms, 'fsdp', 0, 0, tiled=True)  48 us
    all_to_all x1, blocking collectives, on_device(): lax.all_to_all(packed, 'fsdp', 0, 0, axis_index_groups=along_y, tiled=True)  21.3 us
    all_to_all x1, blocking collectives, on_device(): lax.all_to_all(sums, 'cand', 0, 0, axis_index_groups=along_z, tiled=True)  19.3 us
    all_to_all x1, waiting for transfers between devices, on_device(): lax.all_to_all(final, 'cand', 0, 0, axis_index_groups=along_z, tiled=True)  8.57 us
    pallas_call x1, Pallas kernels, on_device(): pl.pallas_call(local_kernel, out_shape=jax.ShapeDtypeStruct((NB, rows, 12...  6.93 us
    pallas_call x1, Pallas kernels, on_device(): pl.pallas_call(near_kernel, out_shape=(jax.ShapeDtypeStruct((HALF, 256),...  5.42 us
    ppermute x1, starting transfers between devices, on_device(): beside = lax.ppermute(pieces, 'cand', sibling)  5.24 us
    ppermute x1, starting transfers between devices, on_device(): other = lax.ppermute(mine, 'cand', sibling)  5.14 us
  transfers between devices with their start and end apart: 6, of which 5 were waited for; matrix products, arithmetic and copies ran while one was open for 0% of the time, Pallas kernels for 4%

profile of v2, /device:TPU:1, one launch (start us, length us, event | category | flops | bytes accessed | tf_op | source)
XLA Modules:
  0.0 150.8 jit_solution(12272130456020677143)
XLA Ops:
  0.6 0.7 fusion
  1.3 0.9 broadcast_select_fusion
  2.3 0.2 shard_map.119
  2.5 21.3 %all_to_all.20.mine_ref = bf16[8,224,128]{2,1,0:T(8,128)(2,1)S(1)} all-to-all(bf16[8,224,128]{2,1,0:T(8,128)(2,1)S(1)} %shard_map.119), channel_id=1, replica_groups={{0,2,4,6,8,10,12,14},{16,18,20,22,24,26,28,30},{1,3,5,7,9,11,13,15},{17..., dimensions={0} | all-to-all | bytes 917504 | tf_op jit(solution)/shard_map/all_to_all | solution.py:305
  23.7 5.1 %collective-permute-start = (bf16[8,224,128]{2,1,0:T(8,128)(2,1)S(1)}, bf16[8,224,128]{2,1,0:T(8,128)(2,1)S(1)}, u32[]{:S(2)}, u32[]{:S(2)}) collective-permute-start(bf16[8,224,128]{2,1,0:T(8,128)(2,1)S(1)} %all_to_all.20.mine_ref), channel_id=1, source_target_pairs={{0,32},{32,0},{64,96},{96,64},{128,160},{160,128},{192,224},{224,1... | collective-permute-start | bytes 1376264 | tf_op jit(solution)/shard_map/ppermute | solution.py:308
  28.9 4.7 %collective-permute-start.1 = (bf16[8,224,128]{2,1,0:T(8,128)(2,1)S(1)}, bf16[8,224,128]{2,1,0:T(8,128)(2,1)S(1)}, u32[]{:S(2)}, u32[]{:S(2)}) collective-permute-start(bf16[8,224,128]{2,1,0:T(8,128)(2,1)S(1)} %all_to_all.20.mine_ref), channel_id=1, source_target_pairs={{0,16},{2,18},{4,20},{6,22},{8,24},{10,26},{12,28},{14,30},{16,0},... | collective-permute-start | bytes 1376264 | tf_op jit(solution)/shard_map/ppermute | solution.py:307
  33.5 0.0 copy-start
  33.6 2.3 %copy-done = bf16[1,1,512,4608]{3,2,1,0:T(8,128)(2,1)S(1)} copy-done((bf16[1,1,512,4608]{3,2,1,0:T(8,128)(2,1)S(1)}, bf16[1,1,512,4608]{3,2,1,0:T(8,128)(2,1)}, u32[]{:S(2)}) %copy-start) | copy-done | bytes 4718616
  35.9 5.4 %shard_map.120 = (bf16[2304,256]{1,0:T(8,128)(2,1)S(1)}, f32[512,256]{1,0:T(8,128)S(1)}, f32[256,256]{1,0:T(8,128)S(1)}, f32[512,128]{1,0:T(8,128)S(1)}) custom-call(bf16[512,4608]{1,0:T(8,128)(2,1)S(1)} %bitcast.9, bf16[8,224,128]{2,1,0:T(8,128)(2,1)S(1)} %all_to_all.20.mine_ref, bf16[8,224,128]{2,1,0:T(8,128)(2,1)S(1)} %collective-permute-done.other_ref), custom_call_target="tpu_custom_call" | custom-call | tf_op jit(solution)/shard_map/pallas_call | solution.py:309
  41.3 3.1 %collective-permute-done.1.mine_ref = bf16[8,224,128]{2,1,0:T(8,128)(2,1)S(1)} collective-permute-done((bf16[8,224,128]{2,1,0:T(8,128)(2,1)S(1)}, bf16[8,224,128]{2,1,0:T(8,128)(2,1)S(1)}, u32[]{:S(2)}, u32[]{:S(2)}) %collective-permute-start.1) | collective-permute-done | bytes 458784 | tf_op jit(solution)/shard_map/ppermute | solution.py:307
  44.4 2.7 %collective-permute-start.2 = (bf16[8,224,128]{2,1,0:T(8,128)(2,1)S(1)}, bf16[8,224,128]{2,1,0:T(8,128)(2,1)S(1)}, u32[]{:S(2)}, u32[]{:S(2)}) collective-permute-start(bf16[8,224,128]{2,1,0:T(8,128)(2,1)S(1)} %collective-permute-done.1.mine_ref), channel_id=1, source_target_pairs={{0,32},{32,0},{64,96},{96,64},{128,160},{160,128},{192,224},{224,1... | collective-permute-start | bytes 1376264 | tf_op jit(solution)/shard_map/ppermute | solution.py:322
  48.4 0.1 collective-permute-done.2.other_ref
  48.5 6.9 %shard_map.121 = s16[16,448,128]{2,1,0:T(8,128)(2,1)S(1)} custom-call(s32[1,1]{1,0:T(1,128)S(6)} %copy.17.starts, s32[1,1]{1,0:T(1,128)S(6)} %copy.16.lengths, bf16[512,4608]{1,0:T(8,128)(2,1)S(1)} %bitcast.10, bf16[2304,256]{1,0:T(8,128)(2,1)S(1)} %get-tuple-element.13.w_near, f32[512,256]{1,0:T(8,128)S(1)} %get-tuple-element.14.prod_near, ...), custom_call_target="tpu_custom_call" | custom-call | tf_op jit(solution)/shard_map/pallas_call | solution.py:324
  55.5 48.0 %all_to_all.21.q_ref = s16[16,448,128]{2,1,0:T(8,128)(2,1)S(1)} all-to-all(s16[16,448,128]{2,1,0:T(8,128)(2,1)S(1)} %shard_map.121), channel_id=1, replica_groups=mesh['cand'=16,'fsdp'=16,'prompt'=2] {'fsdp'}, dimensions={0} | all-to-all | bytes 3670016 | tf_op jit(solution)/shard_map/all_to_all | solution.py:337
  103.5 1.1 shard_map.122
  104.5 0.0 copy-start.4
  104.6 19.3 %all_to_all.22.d_ref = f32[8,64,128]{2,1,0:T(8,128)S(1)} all-to-all(f32[8,64,128]{2,1,0:T(8,128)S(1)} %shard_map.122), channel_id=1, replica_groups={{0,64,128,192,256,320,384,448},{32,96,160,224,288,352,416,480},{1,65,12..., dimensions={0} | all-to-all | bytes 524288 | tf_op jit(solution)/shard_map/all_to_all | solution.py:346
  123.9 5.2 %collective-permute-start.3 = (f32[8,64,128]{2,1,0:T(8,128)S(1)}, f32[8,64,128]{2,1,0:T(8,128)S(1)}, u32[]{:S(2)}, u32[]{:S(2)}) collective-permute-start(f32[8,64,128]{2,1,0:T(8,128)S(1)} %all_to_all.22.d_ref), channel_id=1, source_target_pairs={{0,32},{32,0},{64,96},{96,64},{128,160},{160,128},{192,224},{224,1... | collective-permute-start | bytes 786440 | tf_op jit(solution)/shard_map/ppermute | solution.py:347
  129.1 1.1 collective-permute-done.3.o_ref
  130.3 0.2 shard_map.123
  130.5 2.2 %collective-permute-start.4 = (f32[56,128]{1,0:T(8,128)S(1)}, f32[56,128]{1,0:T(8,128)S(1)}, u32[]{:S(2)}, u32[]{:S(2)}) collective-permute-start(f32[56,128]{1,0:T(8,128)S(1)} %get-tuple-element.20), channel_id=1, source_target_pairs={{0,1},{1,0},{2,3},{3,2},{4,5},{5,4},{6,7},{7,6},{8,9},{9,8},{10,11... | collective-permute-start | bytes 86024 | tf_op jit(solution)/shard_map/ppermute | solution.py:355
  132.8 2.4 %collective-permute-done.4 = f32[56,128]{1,0:T(8,128)S(1)} collective-permute-done((f32[56,128]{1,0:T(8,128)S(1)}, f32[56,128]{1,0:T(8,128)S(1)}, u32[]{:S(2)}, u32[]{:S(2)}) %collective-permute-start.4) | collective-permute-done | bytes 28704 | tf_op jit(solution)/shard_map/ppermute | solution.py:355
  135.1 0.7 broadcast_in_dim.5
  135.8 3.4 %all-to-all-start.3 = ((f32[8,56,128]{2,1,0:T(8,128)}), f32[8,56,128]{2,1,0:T(8,128)S(1)}, u32[]{:S(2)}, u32[]{:S(2)}) async-start(f32[8,56,128]{2,1,0:T(8,128)} %broadcast_in_dim.5), calls=%async_computation.3 | async-start | bytes 458752 | tf_op jit(solution)/shard_map/all_to_all | solution.py:357
  139.2 0.5 slice.27
  139.8 8.6 %all-to-all-done.3 = f32[8,56,128]{2,1,0:T(8,128)S(1)} async-done(((f32[8,56,128]{2,1,0:T(8,128)}), f32[8,56,128]{2,1,0:T(8,128)S(1)}, u32[]{:S(2)}, u32[]{:S(2)}) %all-to-all-start.3) | async-done | bytes 229408 | tf_op jit(solution)/shard_map/all_to_all | solution.py:357
  148.3 0.1 slice.37
  148.5 0.1 fusion.1
  148.6 0.6 convert_multiply_fusion.2
  149.1 0.1 maximum_bitcast_fusion
  149.3 0.8 copy.15
  150.0 0.8 copy.14
  (13 shorter events, 0.1 us)
Async XLA Ops:
  23.7 9.8 %collective-permute-start = (bf16[8,224,128]{2,1,0:T(8,128)(2,1)S(1)}, bf16[8,224,128]{2,1,0:T(8,128)(2,1)S(1)}, u32[]{:S(2)}, u32[]{:S(2)}) collective-permute-start(bf16[8,224,128]{2,1,0:T(8,128)(2,1)S(1)} %all_to_all.20.mine_ref), channel_id=1, source_target_pairs={{0,32},{32,0},{64,96},{96,64},{128,160},{160,128},{192,224},{224,1... | collective-permute-start | bytes 1376264 | tf_op jit(solution)/shard_map/ppermute | solution.py:308
  28.9 15.5 %collective-permute-start.1 = (bf16[8,224,128]{2,1,0:T(8,128)(2,1)S(1)}, bf16[8,224,128]{2,1,0:T(8,128)(2,1)S(1)}, u32[]{:S(2)}, u32[]{:S(2)}) collective-permute-start(bf16[8,224,128]{2,1,0:T(8,128)(2,1)S(1)} %all_to_all.20.mine_ref), channel_id=1, source_target_pairs={{0,16},{2,18},{4,20},{6,22},{8,24},{10,26},{12,28},{14,30},{16,0},... | collective-permute-start | bytes 1376264 | tf_op jit(solution)/shard_map/ppermute | solution.py:307
  33.5 2.3 %copy-start = (bf16[1,1,512,4608]{3,2,1,0:T(8,128)(2,1)S(1)}, bf16[1,1,512,4608]{3,2,1,0:T(8,128)(2,1)}, u32[]{:S(2)}) copy-start(bf16[1,1,512,4608]{3,2,1,0:T(8,128)(2,1)} %param.8) | copy-start | bytes 14155780
  35.9 12.7 %copy-start.1 = (bf16[1,1,512,4608]{3,2,1,0:T(8,128)(2,1)S(1)}, bf16[1,1,512,4608]{3,2,1,0:T(8,128)(2,1)}, u32[]{:S(2)}) copy-start(bf16[1,1,512,4608]{3,2,1,0:T(8,128)(2,1)} %param.8) | copy-start | bytes 14155780
  44.4 4.1 %collective-permute-start.2 = (bf16[8,224,128]{2,1,0:T(8,128)(2,1)S(1)}, bf16[8,224,128]{2,1,0:T(8,128)(2,1)S(1)}, u32[]{:S(2)}, u32[]{:S(2)}) collective-permute-start(bf16[8,224,128]{2,1,0:T(8,128)(2,1)S(1)} %collective-permute-done.1.mine_ref), channel_id=1, source_target_pairs={{0,32},{32,0},{64,96},{96,64},{128,160},{160,128},{192,224},{224,1... | collective-permute-start | bytes 1376264 | tf_op jit(solution)/shard_map/ppermute | solution.py:322
  55.5 48.0 %copy-start.2 = (s32[1,16]{1,0:T(1,128)S(1)}, s32[1,16]{1,0:T(1,128)}, u32[]{:S(2)}) copy-start(s32[1,16]{1,0:T(1,128)} %ranking.1) | copy-start | bytes 196
  104.5 44.0 %copy-start.3 = (bf16[288]{0:T(512)(128)(2,1)S(1)}, bf16[288]{0:T(512)(128)(2,1)}, u32[]{:S(2)}) copy-start(bf16[288]{0:T(512)(128)(2,1)} %param.15) | copy-start | bytes 1732
  104.5 44.0 %copy-start.4 = (bf16[288]{0:T(512)(128)(2,1)S(1)}, bf16[288]{0:T(512)(128)(2,1)}, u32[]{:S(2)}) copy-start(bf16[288]{0:T(512)(128)(2,1)} %param.14) | copy-start | bytes 1732
  123.9 6.4 %collective-permute-start.3 = (f32[8,64,128]{2,1,0:T(8,128)S(1)}, f32[8,64,128]{2,1,0:T(8,128)S(1)}, u32[]{:S(2)}, u32[]{:S(2)}) collective-permute-start(f32[8,64,128]{2,1,0:T(8,128)S(1)} %all_to_all.22.d_ref), channel_id=1, source_target_pairs={{0,32},{32,0},{64,96},{96,64},{128,160},{160,128},{192,224},{224,1... | collective-permute-start | bytes 786440 | tf_op jit(solution)/shard_map/ppermute | solution.py:347
  130.5 4.6 %collective-permute-start.4 = (f32[56,128]{1,0:T(8,128)S(1)}, f32[56,128]{1,0:T(8,128)S(1)}, u32[]{:S(2)}, u32[]{:S(2)}) collective-permute-start(f32[56,128]{1,0:T(8,128)S(1)} %get-tuple-element.20), channel_id=1, source_target_pairs={{0,1},{1,0},{2,3},{3,2},{4,5},{5,4},{6,7},{7,6},{8,9},{9,8},{10,11... | collective-permute-start | bytes 86024 | tf_op jit(solution)/shard_map/ppermute | solution.py:355
  135.8 12.5 %all-to-all-start.3 = ((f32[8,56,128]{2,1,0:T(8,128)}), f32[8,56,128]{2,1,0:T(8,128)S(1)}, u32[]{:S(2)}, u32[]{:S(2)}) async-start(f32[8,56,128]{2,1,0:T(8,128)} %broadcast_in_dim.5), calls=%async_computation.3 | async-start | bytes 458752 | tf_op jit(solution)/shard_map/all_to_all | solution.py:357

commit v3 on v2

--- a/solution.py
+++ b/solution.py
@@ -13,6 +13,7 @@
 BW = 288
 HALF = 2304
 CH = 512
+CUT = 224
 STEPS = 32760.0
 FINE = 60000.0
 TINY = 1e-36
@@ -41,6 +42,41 @@
 
 def coded(v, e):
     return jnp.round(v * jnp.exp2(e * -0.125) * STEPS).astype(jnp.int32)
+
+
+def told_row(part):
+    e = level(jnp.abs(part))
+    v = part * jnp.exp2(e * -0.125) * STEPS
+    hi = jnp.round(v)
+    lo = jnp.round((v - hi) * FINE)
+    one = lanes((1, 128))
+    return jnp.where(one == 0, e, jnp.where(one == 1, hi, jnp.where(one == 2, lo, 0.0))).astype(jnp.int32)
+
+
+def told(m, scale):
+    one = lanes((1, 128))
+    v = jnp.where(one == 1, m[6:7], jnp.where(one == 2, m[6:7] * (1.0 / FINE), 0.0))
+    by = jnp.sum(jnp.where(one == 0, scale[6:7], 0.0), axis=1, keepdims=True)
+    return jnp.sum(v, axis=1, keepdims=True) * (by * (1.0 / STEPS))
+
+
+def meta_rows(a_e, b_e, window, s_row):
+    p_e = level(jnp.max(jnp.abs(window), axis=1, keepdims=True))
+    p_q = coded(window, p_e)
+    rows = (
+        a_e.astype(jnp.int32),
+        b_e.astype(jnp.int32),
+        p_q[0:1, :128],
+        p_q[0:1, 128:256],
+        p_q[0:1, 256:384],
+        jnp.broadcast_to(p_e[0:1].astype(jnp.int32), (1, 128)),
+        s_row,
+    )
+    at = lax.broadcasted_iota(jnp.int32, (16, 128), 0)
+    meta = jnp.zeros((16, 128), jnp.int32)
+    for k, r in enumerate(rows):
+        meta = jnp.where(at == k, r, meta)
+    return meta.astype(jnp.int16)
 
 
 def pack_kernel(w_ref, out_ref):
@@ -115,7 +151,25 @@
 
 
 def local_kernel(
-    starts, lengths, x_ref, w_near, prod_near, gram_near, ss_ref, mine_ref, other_ref, out_ref, w_far, w_ref, g_ref, p_ref
+    starts,
+    lengths,
+    x_ref,
+    w_near,
+    prod_near,
+    gram_near,
+    ss_ref,
+    mine_ref,
+    other_ref,
+    send_a,
+    send_b,
+    own_a,
+    own_b,
+    own_p,
+    own_s,
+    w_far,
+    w_ref,
+    g_ref,
+    p_ref,
 ):
     start, length = starts[0, 0], lengths[0, 0]
     first = lax.axis_index("fsdp") * TOK
@@ -182,43 +236,65 @@
     p_ref[:, D:] = jnp.zeros((8, 256), f32)
     p_ref[:, :D] = jnp.broadcast_to(pooled[0:1] + pooled[1:2], (8, D))
 
-    s_e = level(jnp.abs(part))
-    s_v = part * jnp.exp2(s_e * -0.125) * STEPS
-    s_hi = jnp.round(s_v)
-    s_lo = jnp.round((s_v - s_hi) * FINE)
-    one = lanes((1, 128))
-    s_row = jnp.where(one == 0, s_e, jnp.where(one == 1, s_hi, jnp.where(one == 2, s_lo, 0.0))).astype(jnp.int32)
-    for j in range(NB):
-        a = g_ref[j * BW : (j + 1) * BW, :128]
-        b0 = g_ref[j * BW : j * BW + BW // 2, 128:]
-        b1 = g_ref[j * BW + BW // 2 : (j + 1) * BW, 128:]
-        b = jnp.where(lanes((BW // 2, 128)) < 64, b0, b1)
+    def window(j):
+        base = j * BW // 128 * 128
+        off = j * BW - base
+        w = p_ref[:, base : base + 512]
+        if off:
+            w = pltpu.roll(w, 512 - off, 1)
+        return jnp.where(lanes((8, 512)) < BW, w, 0.0)
+
+    def block(j):
+        a = g_ref[pl.ds(pl.multiple_of(j * BW, 32), BW), :128]
+        b0 = g_ref[pl.ds(pl.multiple_of(j * BW, 32), BW // 2), 128:]
+        b1 = g_ref[pl.ds(pl.multiple_of(j * BW + BW // 2, 16), BW // 2), 128:]
+        return a, jnp.where(lanes((BW // 2, 128)) < 64, b0, b1)
+
+    par = lax.axis_index("fsdp") % 2
+    s_row = told_row(part)
+    own_s[...] = jnp.broadcast_to(part, (8, 128))
+    for i in range(8):
+        even, odd = window(2 * i), window(2 * i + 1)
+        a, b = block(2 * i + 1 - par)
         a_e = level(jnp.max(jnp.abs(a), axis=0, keepdims=True))
         b_e = level(jnp.max(jnp.abs(b), axis=0, keepdims=True))
-        out_ref[j, :BW, :] = coded(a, a_e).astype(jnp.int16)
-        out_ref[j, BW : BW + BW // 2, :] = coded(b, b_e).astype(jnp.int16)
-        base = j * BW // 128 * 128
-        window = p_ref[:, base : base + 512]
-        off = j * BW - base
-        if off:
-            window = pltpu.roll(window, 512 - off, 1)
-        window = jnp.where(lanes((8, 512)) < BW, window, 0.0)
-        p_e = level(jnp.max(jnp.abs(window), axis=1, keepdims=True))
-        p_q = coded(window, p_e)
-        at = lax.broadcasted_iota(jnp.int32, (16, 128), 0)
-        rows = (
-            a_e.astype(jnp.int32),
-            b_e.astype(jnp.int32),
-            p_q[0:1, :128],
-            p_q[0:1, 128:256],
-            p_q[0:1, 256:384],
-            jnp.broadcast_to(p_e[0:1].astype(jnp.int32), (1, 128)),
-            s_row,
+        q = coded(a, a_e).astype(jnp.int16)
+        meta = meta_rows(a_e, b_e, jnp.where(par == 0, odd, even), s_row)
+        send_a[i, :CUT, :] = q[:CUT]
+        send_a[i, CUT:, :] = meta
+        send_b[i, : BW - CUT, :] = q[CUT:]
+        send_b[i, BW - CUT : BW - CUT + BW // 2, :] = coded(b, b_e).astype(jnp.int16)
+        send_b[i, BW - CUT + BW // 2 :, :] = meta
+        a, b = block(2 * i + par)
+        own_a[i] = a
+        own_b[i] = b
+        own_p[i] = jnp.where(par == 0, even, odd)
+
+
+def pair_kernel(got_a, got_b, own_a, own_b, own_p, own_s, out_ref):
+    end = BW - CUT + BW // 2
+    m_a = [got_a[i, CUT:, :].astype(jnp.int32).astype(f32) for i in range(8)]
+    m_b = [got_b[i, end:, :].astype(jnp.int32).astype(f32) for i in range(8)]
+    scale = jnp.exp2(m_b[0] * 0.125)
+    s_row = told_row(own_s[0:1, 0:1] + told(m_b[0], scale))
+    for i in range(8):
+        by_a = jnp.exp2(m_a[i][0:1] * 0.125) * (1.0 / STEPS)
+        by = jnp.exp2(m_b[i] * 0.125) * (1.0 / STEPS)
+        top = own_a[i, :CUT] + got_a[i, :CUT, :].astype(jnp.int32).astype(f32) * by_a
+        low = own_a[i, CUT:] + got_b[i, : BW - CUT, :].astype(jnp.int32).astype(f32) * by[0:1]
+        b = own_b[i] + got_b[i, BW - CUT : end, :].astype(jnp.int32).astype(f32) * by[1:2]
+        m = m_b[i]
+        got_p = jnp.concatenate([m[2:3], m[3:4], m[4:5], jnp.zeros((1, 128), f32)], axis=1)
+        p = own_p[i] + got_p * jnp.concatenate([by[5:6]] * 4, axis=1)
+        most = jnp.maximum(
+            jnp.max(jnp.abs(top), axis=0, keepdims=True), jnp.max(jnp.abs(low), axis=0, keepdims=True)
         )
-        meta = jnp.zeros((16, 128), jnp.int32)
-        for k, r in enumerate(rows):
-            meta = jnp.where(at == k, r, meta)
-        out_ref[j, BW + BW // 2 :, :] = meta.astype(jnp.int16)
+        a_e = level(most)
+        b_e = level(jnp.max(jnp.abs(b), axis=0, keepdims=True))
+        out_ref[i, :CUT, :] = coded(top, a_e).astype(jnp.int16)
+        out_ref[i, CUT:BW, :] = coded(low, a_e).astype(jnp.int16)
+        out_ref[i, BW : BW + BW // 2, :] = coded(b, b_e).astype(jnp.int16)
+        out_ref[i, BW + BW // 2 :, :] = meta_rows(a_e, b_e, p, s_row)
 
 
 def block_kernel(ranking, q_ref, out_ref):
@@ -227,19 +303,16 @@
     for k in range(16):
         place = jnp.where(ranking[0, k] == mine, jnp.int32(k), place)
     half = BW + BW // 2
-    parts = [q_ref[s, half:, :].astype(jnp.int32).astype(f32) for s in range(NB)]
+    parts = [q_ref[s, half:, :].astype(jnp.int32).astype(f32) for s in range(8)]
     scale = [jnp.exp2(m * 0.125) for m in parts]
     pooled = [jnp.zeros((1, 128), f32) for _ in range(3)]
-    reward = jnp.zeros((1, 128), f32)
+    reward = jnp.zeros((1, 1), f32)
     one = lanes((1, 128))
-    for s in range(NB):
+    for s in range(8):
         m, e = parts[s], scale[s] * (1.0 / STEPS)
         for k in range(3):
             pooled[k] = pooled[k] + m[2 + k : 3 + k] * e[5:6]
-        told = jnp.where(one == 1, m[6:7], jnp.where(one == 2, m[6:7] * (1.0 / FINE), 0.0))
-        told = jnp.sum(told, axis=1, keepdims=True)
-        by = jnp.sum(jnp.where(one == 0, e[6:7], 0.0), axis=1, keepdims=True)
-        reward = reward + told * by
+        reward = reward + told(m, scale[s])
     at = lax.broadcasted_iota(jnp.int32, (16, 128), 0)
     tail = jnp.zeros((16, 128), f32)
     for k in range(3):
@@ -250,7 +323,7 @@
         if i < half // 16:
             which = 0 if i < BW // 16 else 1
             acc = jnp.zeros((16, 128), f32)
-            for s in range(NB):
+            for s in range(8):
                 v = q_ref[s, i * 16 : (i + 1) * 16, :].astype(jnp.int32).astype(f32)
                 acc = acc + v * (scale[s][which : which + 1] * (1.0 / STEPS))
         else:
@@ -321,11 +394,18 @@
     far_mine, squares = lax.optimization_barrier((far_mine, squares))
     far_other = lax.ppermute(far_mine, "cand", sibling)
     rows = BW + BW // 2 + 16
-    coded_terms = pl.pallas_call(
+    send_a, send_b, *own = pl.pallas_call(
         local_kernel,
-        out_shape=jax.ShapeDtypeStruct((NB, rows, 128), jnp.int16),
+        out_shape=(
+            jax.ShapeDtypeStruct((8, CUT + 16, 128), jnp.int16),
+            jax.ShapeDtypeStruct((8, rows - CUT, 128), jnp.int16),
+            jax.ShapeDtypeStruct((8, BW, 128), f32),
+            jax.ShapeDtypeStruct((8, BW // 2, 128), f32),
+            jax.ShapeDtypeStruct((8, 8, 512), f32),
+            jax.ShapeDtypeStruct((8, 128), f32),
+        ),
         in_specs=[SMEM, SMEM] + [VMEM] * 7,
-        out_specs=VMEM,
+        out_specs=(VMEM,) * 6,
         scratch_shapes=[
             pltpu.VMEM((HALF, 256), bf16),
             pltpu.VMEM((D, 256), bf16),
@@ -334,7 +414,18 @@
         ],
         compiler_params=pltpu.CompilerParams(vmem_limit_bytes=40 << 20),
     )(starts, lengths, x, w_near, prod, gram, squares, far_mine, far_other)
-    swapped = lax.all_to_all(coded_terms, "fsdp", 0, 0, tiled=True)
+    got_a = lax.ppermute(send_a, "fsdp", [(i, i ^ 1) for i in range(16)])
+    turn = [(i, i // 8 * 8 + (i + (1 if i % 2 else 7)) % 8) for i in range(16)]
+    got_b = lax.ppermute(send_b, "fsdp", turn)
+    coded_terms = pl.pallas_call(
+        pair_kernel,
+        out_shape=jax.ShapeDtypeStruct((8, rows, 128), jnp.int16),
+        in_specs=[VMEM] * 6,
+        out_specs=VMEM,
+        compiler_params=pltpu.CompilerParams(vmem_limit_bytes=24 << 20),
+    )(got_a, got_b, *own)
+    parity = [list(range(0, 16, 2)), list(range(1, 16, 2))]
+    swapped = lax.all_to_all(coded_terms, "fsdp", 0, 0, axis_index_groups=parity, tiled=True)
     sums = pl.pallas_call(
         block_kernel,
         out_shape=jax.ShapeDtypeStruct((8, 64, 128), f32),

time: 154 us -> 154 us (level)
  blocking collectives: 88.6 us -> 71.1 us
  waiting for transfers between devices: 15.3 us -> 27.8 us
  starting transfers between devices: 23.4 us -> 27.7 us
    all_to_all x1, blocking collectives: 48 us -> 30.5 us  [on_device(): lax.all_to_all(coded_terms, 'fsdp', 0, 0, axis_index_groups=parity, tiled...]
    ppermute x0 -> x2, waiting for transfers between devices: none -> 12.5 us  [the longest x1 12.5 us: on_device(): got_b = lax.ppermute(send_b, 'fsdp', turn)]
    ppermute x0 -> x2, starting transfers between devices: none -> 4.16 us  [the longest x1 2.19 us: on_device(): got_a = lax.ppermute(send_a, 'fsdp', [(i, i ^ 1) for i in range(16)])]
    pallas_call x1 -> x2, Pallas kernels: 6.93 us -> 8.01 us  [the longest x1 7.37 us: on_device(): pl.pallas_call(local_kernel, out_shape=(jax.ShapeDtypeStruct((8, CUT + 16...]
  transfers between devices with their start and end apart: 6 -> 8, of which waited for: 5 -> 6; matrix products, arithmetic and copies ran while one was open for 0% -> 0% of each run, Pallas kernels for 4% -> 4%
where the time goes in v3:
time: 154 us; the launch traced here: 151 us
  blocking collectives  71.1 us (46%)
  waiting for transfers between devices  27.8 us (18%)
  starting transfers between devices  27.7 us (18%)
  Pallas kernels  14.6 us (9%)
  local copies, waits for them, and re-layouts  5.33 us (3%)
  other arithmetic  2.32 us (2%)
  between operations  2.13 us (1%)
    all_to_all x1, blocking collectives, on_device(): lax.all_to_all(coded_terms, 'fsdp', 0, 0, axis_index_groups=parity, tiled...  30.5 us
    all_to_all x1, blocking collectives, on_device(): lax.all_to_all(packed, 'fsdp', 0, 0, axis_index_groups=along_y, tiled=True)  21.3 us
    all_to_all x1, blocking collectives, on_device(): lax.all_to_all(sums, 'cand', 0, 0, axis_index_groups=along_z, tiled=True)  19.3 us
    ppermute x1, waiting for transfers between devices, on_device(): got_b = lax.ppermute(send_b, 'fsdp', turn)  12.5 us
    all_to_all x1, waiting for transfers between devices, on_device(): lax.all_to_all(final, 'cand', 0, 0, axis_index_groups=along_z, tiled=True)  8.57 us
    pallas_call x1, Pallas kernels, on_device(): pl.pallas_call(local_kernel, out_shape=(jax.ShapeDtypeStruct((8, CUT + 16...  7.37 us
    pallas_call x1, Pallas kernels, on_device(): pl.pallas_call(near_kernel, out_shape=(jax.ShapeDtypeStruct((HALF, 256),...  5.42 us
    ppermute x1, starting transfers between devices, on_device(): beside = lax.ppermute(pieces, 'cand', sibling)  5.38 us
  transfers between devices with their start and end apart: 8, of which 6 were waited for; matrix products, arithmetic and copies ran while one was open for 0% of the time, Pallas kernels for 4%

profile of v3, /device:TPU:1, one launch (start us, length us, event | category | flops | bytes accessed | tf_op | source)
XLA Modules:
  0.0 151.0 jit_solution(9453211354781198166)
XLA Ops:
  0.6 0.7 fusion
  1.3 0.9 broadcast_select_fusion
  2.3 0.2 shard_map.119
  2.5 21.3 %all_to_all.20.mine_ref = bf16[8,224,128]{2,1,0:T(8,128)(2,1)S(1)} all-to-all(bf16[8,224,128]{2,1,0:T(8,128)(2,1)S(1)} %shard_map.119), channel_id=1, replica_groups={{0,2,4,6,8,10,12,14},{16,18,20,22,24,26,28,30},{1,3,5,7,9,11,13,15},{17..., dimensions={0} | all-to-all | bytes 917504 | tf_op jit(solution)/shard_map/all_to_all | solution.py:378
  23.7 5.1 %collective-permute-start = (bf16[8,224,128]{2,1,0:T(8,128)(2,1)S(1)}, bf16[8,224,128]{2,1,0:T(8,128)(2,1)S(1)}, u32[]{:S(2)}, u32[]{:S(2)}) collective-permute-start(bf16[8,224,128]{2,1,0:T(8,128)(2,1)S(1)} %all_to_all.20.mine_ref), channel_id=1, source_target_pairs={{0,32},{32,0},{64,96},{96,64},{128,160},{160,128},{192,224},{224,1... | collective-permute-start | bytes 1376264 | tf_op jit(solution)/shard_map/ppermute | solution.py:381
  28.9 4.7 %collective-permute-start.1 = (bf16[8,224,128]{2,1,0:T(8,128)(2,1)S(1)}, bf16[8,224,128]{2,1,0:T(8,128)(2,1)S(1)}, u32[]{:S(2)}, u32[]{:S(2)}) collective-permute-start(bf16[8,224,128]{2,1,0:T(8,128)(2,1)S(1)} %all_to_all.20.mine_ref), channel_id=1, source_target_pairs={{0,16},{2,18},{4,20},{6,22},{8,24},{10,26},{12,28},{14,30},{16,0},... | collective-permute-start | bytes 1376264 | tf_op jit(solution)/shard_map/ppermute | solution.py:380
  33.6 2.3 %copy-done = bf16[1,1,512,4608]{3,2,1,0:T(8,128)(2,1)S(1)} copy-done((bf16[1,1,512,4608]{3,2,1,0:T(8,128)(2,1)S(1)}, bf16[1,1,512,4608]{3,2,1,0:T(8,128)(2,1)}, u32[]{:S(2)}) %copy-start) | copy-done | bytes 4718616
  35.9 5.4 %shard_map.120 = (bf16[2304,256]{1,0:T(8,128)(2,1)S(1)}, f32[512,256]{1,0:T(8,128)S(1)}, f32[256,256]{1,0:T(8,128)S(1)}, f32[512,128]{1,0:T(8,128)S(1)}) custom-call(bf16[512,4608]{1,0:T(8,128)(2,1)S(1)} %bitcast.9, bf16[8,224,128]{2,1,0:T(8,128)(2,1)S(1)} %all_to_all.20.mine_ref, bf16[8,224,128]{2,1,0:T(8,128)(2,1)S(1)} %collective-permute-done.other_ref), custom_call_target="tpu_custom_call" | custom-call | tf_op jit(solution)/shard_map/pallas_call | solution.py:382
  41.3 3.1 %collective-permute-done.1.mine_ref = bf16[8,224,128]{2,1,0:T(8,128)(2,1)S(1)} collective-permute-done((bf16[8,224,128]{2,1,0:T(8,128)(2,1)S(1)}, bf16[8,224,128]{2,1,0:T(8,128)(2,1)S(1)}, u32[]{:S(2)}, u32[]{:S(2)}) %collective-permute-start.1) | collective-permute-done | bytes 458784 | tf_op jit(solution)/shard_map/ppermute | solution.py:380
  44.4 2.7 %collective-permute-start.2 = (bf16[8,224,128]{2,1,0:T(8,128)(2,1)S(1)}, bf16[8,224,128]{2,1,0:T(8,128)(2,1)S(1)}, u32[]{:S(2)}, u32[]{:S(2)}) collective-permute-start(bf16[8,224,128]{2,1,0:T(8,128)(2,1)S(1)} %collective-permute-done.1.mine_ref), channel_id=1, source_target_pairs={{0,32},{32,0},{64,96},{96,64},{128,160},{160,128},{192,224},{224,1... | collective-permute-start | bytes 1376264 | tf_op jit(solution)/shard_map/ppermute | solution.py:395
  48.4 0.1 collective-permute-done.2.other_ref
  48.5 7.4 %shard_map.121 = (s16[8,240,128]{2,1,0:T(8,128)(2,1)S(1)}, s16[8,224,128]{2,1,0:T(8,128)(2,1)S(1)}, f32[8,288,128]{2,1,0:T(8,128)S(1)}, f32[8,144,128]{2,1,0:T(8...) custom-call(s32[1,1]{1,0:T(1,128)S(6)} %copy.17.starts, s32[1,1]{1,0:T(1,128)S(6)} %copy.16.lengths, ...), custom_call_target="tpu_custom_call" | custom-call | tf_op jit(solution)/shard_map/pallas_call | solution.py:397
  55.9 2.2 %collective-permute-start.3 = (s16[8,240,128]{2,1,0:T(8,128)(2,1)S(1)}, s16[8,240,128]{2,1,0:T(8,128)(2,1)S(1)}, u32[]{:S(2)}, u32[]{:S(2)}) collective-permute-start(s16[8,240,128]{2,1,0:T(8,128)(2,1)S(1)} %get-tuple-element.25), channel_id=1, source_target_pairs={{0,2},{2,0},{4,6},{6,4},{8,10},{10,8},{12,14},{14,12},{16,18},{18,... | collective-permute-start | bytes 1474568 | tf_op jit(solution)/shard_map/ppermute | solution.py:417
  58.1 2.0 %collective-permute-start.4 = (s16[8,224,128]{2,1,0:T(8,128)(2,1)S(1)}, s16[8,224,128]{2,1,0:T(8,128)(2,1)S(1)}, u32[]{:S(2)}, u32[]{:S(2)}) collective-permute-start(s16[8,224,128]{2,1,0:T(8,128)(2,1)S(1)} %get-tuple-element.26), channel_id=1, source_target_pairs={{0,14},{2,4},{4,2},{6,8},{8,6},{10,12},{12,10},{14,0},{16,30},{18,... | collective-permute-start | bytes 1376264 | tf_op jit(solution)/shard_map/ppermute | solution.py:419
  60.1 12.5 %collective-permute-done.4.got_b = s16[8,224,128]{2,1,0:T(8,128)(2,1)S(1)} collective-permute-done((s16[8,224,128]{2,1,0:T(8,128)(2,1)S(1)}, s16[8,224,128]{2,1,0:T(8,128)(2,1)S(1)}, u32[]{:S(2)}, u32[]{:S(2)}) %collective-permute-start.4) | collective-permute-done | bytes 458784 | tf_op jit(solution)/shard_map/ppermute | solution.py:419
  72.6 0.6 shard_map.122
  73.3 30.5 %all_to_all.21.q_ref = s16[8,448,128]{2,1,0:T(8,128)(2,1)S(1)} all-to-all(s16[8,448,128]{2,1,0:T(8,128)(2,1)S(1)} %shard_map.122), channel_id=1, replica_groups={{0,4,8,12,16,20,24,28},{2,6,10,14,18,22,26,30},{1,5,9,13,17,21,25,29},{..., dimensions={0} | all-to-all | bytes 1835008 | tf_op jit(solution)/shard_map/all_to_all | solution.py:428
  103.8 0.8 shard_map.123
  104.6 19.3 %all_to_all.22.d_ref = f32[8,64,128]{2,1,0:T(8,128)S(1)} all-to-all(f32[8,64,128]{2,1,0:T(8,128)S(1)} %shard_map.123), channel_id=1, replica_groups={{0,64,128,192,256,320,384,448},{32,96,160,224,288,352,416,480},{1,65,12..., dimensions={0} | all-to-all | bytes 524288 | tf_op jit(solution)/shard_map/all_to_all | solution.py:437
  124.0 5.4 %collective-permute-start.5 = (f32[8,64,128]{2,1,0:T(8,128)S(1)}, f32[8,64,128]{2,1,0:T(8,128)S(1)}, u32[]{:S(2)}, u32[]{:S(2)}) collective-permute-start(f32[8,64,128]{2,1,0:T(8,128)S(1)} %all_to_all.22.d_ref), channel_id=1, source_target_pairs={{0,32},{32,0},{64,96},{96,64},{128,160},{160,128},{192,224},{224,1... | collective-permute-start | bytes 786440 | tf_op jit(solution)/shard_map/ppermute | solution.py:438
  129.3 1.1 collective-permute-done.5.o_ref
  130.5 0.2 shard_map.124
  130.7 2.2 %collective-permute-start.6 = (f32[56,128]{1,0:T(8,128)S(1)}, f32[56,128]{1,0:T(8,128)S(1)}, u32[]{:S(2)}, u32[]{:S(2)}) collective-permute-start(f32[56,128]{1,0:T(8,128)S(1)} %get-tuple-element.32), channel_id=1, source_target_pairs={{0,1},{1,0},{2,3},{3,2},{4,5},{5,4},{6,7},{7,6},{8,9},{9,8},{10,11... | collective-permute-start | bytes 86024 | tf_op jit(solution)/shard_map/ppermute | solution.py:446
  133.0 2.4 %collective-permute-done.6 = f32[56,128]{1,0:T(8,128)S(1)} collective-permute-done((f32[56,128]{1,0:T(8,128)S(1)}, f32[56,128]{1,0:T(8,128)S(1)}, u32[]{:S(2)}, u32[]{:S(2)}) %collective-permute-start.6) | collective-permute-done | bytes 28704 | tf_op jit(solution)/shard_map/ppermute | solution.py:446
  135.3 0.7 broadcast_in_dim.5
  136.1 3.4 %all-to-all-start.3 = ((f32[8,56,128]{2,1,0:T(8,128)}), f32[8,56,128]{2,1,0:T(8,128)S(1)}, u32[]{:S(2)}, u32[]{:S(2)}) async-start(f32[8,56,128]{2,1,0:T(8,128)} %broadcast_in_dim.5), calls=%async_computation.3 | async-start | bytes 458752 | tf_op jit(solution)/shard_map/all_to_all | solution.py:448
  139.5 0.5 slice.27
  140.0 8.6 %all-to-all-done.3 = f32[8,56,128]{2,1,0:T(8,128)S(1)} async-done(((f32[8,56,128]{2,1,0:T(8,128)}), f32[8,56,128]{2,1,0:T(8,128)S(1)}, u32[]{:S(2)}, u32[]{:S(2)}) %all-to-all-start.3) | async-done | bytes 229408 | tf_op jit(solution)/shard_map/all_to_all | solution.py:448
  148.8 0.6 convert_multiply_fusion.2
  149.4 0.1 maximum_bitcast_fusion
  149.5 0.8 copy.15
  150.3 0.8 copy.14
  (18 shorter events, 0.2 us)
Async XLA Ops:
  23.7 9.8 %collective-permute-start = (bf16[8,224,128]{2,1,0:T(8,128)(2,1)S(1)}, bf16[8,224,128]{2,1,0:T(8,128)(2,1)S(1)}, u32[]{:S(2)}, u32[]{:S(2)}) collective-permute-start(bf16[8,224,128]{2,1,0:T(8,128)(2,1)S(1)} %all_to_all.20.mine_ref), channel_id=1, source_target_pairs={{0,32},{32,0},{64,96},{96,64},{128,160},{160,128},{192,224},{224,1... | collective-permute-start | bytes 1376264 | tf_op jit(solution)/shard_map/ppermute | solution.py:381
  28.9 15.5 %collective-permute-start.1 = (bf16[8,224,128]{2,1,0:T(8,128)(2,1)S(1)}, bf16[8,224,128]{2,1,0:T(8,128)(2,1)S(1)}, u32[]{:S(2)}, u32[]{:S(2)}) collective-permute-start(bf16[8,224,128]{2,1,0:T(8,128)(2,1)S(1)} %all_to_all.20.mine_ref), channel_id=1, source_target_pairs={{0,16},{2,18},{4,20},{6,22},{8,24},{10,26},{12,28},{14,30},{16,0},... | collective-permute-start | bytes 1376264 | tf_op jit(solution)/shard_map/ppermute | solution.py:380
  33.5 2.3 %copy-start = (bf16[1,1,512,4608]{3,2,1,0:T(8,128)(2,1)S(1)}, bf16[1,1,512,4608]{3,2,1,0:T(8,128)(2,1)}, u32[]{:S(2)}) copy-start(bf16[1,1,512,4608]{3,2,1,0:T(8,128)(2,1)} %param.8) | copy-start | bytes 14155780
  35.9 12.7 %copy-start.1 = (bf16[1,1,512,4608]{3,2,1,0:T(8,128)(2,1)S(1)}, bf16[1,1,512,4608]{3,2,1,0:T(8,128)(2,1)}, u32[]{:S(2)}) copy-start(bf16[1,1,512,4608]{3,2,1,0:T(8,128)(2,1)} %param.8) | copy-start | bytes 14155780
  44.4 4.1 %collective-permute-start.2 = (bf16[8,224,128]{2,1,0:T(8,128)(2,1)S(1)}, bf16[8,224,128]{2,1,0:T(8,128)(2,1)S(1)}, u32[]{:S(2)}, u32[]{:S(2)}) collective-permute-start(bf16[8,224,128]{2,1,0:T(8,128)(2,1)S(1)} %collective-permute-done.1.mine_ref), channel_id=1, source_target_pairs={{0,32},{32,0},{64,96},{96,64},{128,160},{160,128},{192,224},{224,1... | collective-permute-start | bytes 1376264 | tf_op jit(solution)/shard_map/ppermute | solution.py:395
  55.9 16.7 %collective-permute-start.3 = (s16[8,240,128]{2,1,0:T(8,128)(2,1)S(1)}, s16[8,240,128]{2,1,0:T(8,128)(2,1)S(1)}, u32[]{:S(2)}, u32[]{:S(2)}) collective-permute-start(s16[8,240,128]{2,1,0:T(8,128)(2,1)S(1)} %get-tuple-element.25), channel_id=1, source_target_pairs={{0,2},{2,0},{4,6},{6,4},{8,10},{10,8},{12,14},{14,12},{16,18},{18,... | collective-permute-start | bytes 1474568 | tf_op jit(solution)/shard_map/ppermute | solution.py:417
  58.1 14.5 %collective-permute-start.4 = (s16[8,224,128]{2,1,0:T(8,128)(2,1)S(1)}, s16[8,224,128]{2,1,0:T(8,128)(2,1)S(1)}, u32[]{:S(2)}, u32[]{:S(2)}) collective-permute-start(s16[8,224,128]{2,1,0:T(8,128)(2,1)S(1)} %get-tuple-element.26), channel_id=1, source_target_pairs={{0,14},{2,4},{4,2},{6,8},{8,6},{10,12},{12,10},{14,0},{16,30},{18,... | collective-permute-start | bytes 1376264 | tf_op jit(solution)/shard_map/ppermute | solution.py:419
  73.3 30.5 %copy-start.2 = (s32[1,16]{1,0:T(1,128)S(1)}, s32[1,16]{1,0:T(1,128)}, u32[]{:S(2)}) copy-start(s32[1,16]{1,0:T(1,128)} %ranking.1) | copy-start | bytes 196
  124.0 24.8 %copy-start.3 = (bf16[288]{0:T(512)(128)(2,1)S(1)}, bf16[288]{0:T(512)(128)(2,1)}, u32[]{:S(2)}) copy-start(bf16[288]{0:T(512)(128)(2,1)} %param.15) | copy-start | bytes 1732
  124.0 24.8 %copy-start.4 = (bf16[288]{0:T(512)(128)(2,1)S(1)}, bf16[288]{0:T(512)(128)(2,1)}, u32[]{:S(2)}) copy-start(bf16[288]{0:T(512)(128)(2,1)} %param.14) | copy-start | bytes 1732
  124.0 6.5 %collective-permute-start.5 = (f32[8,64,128]{2,1,0:T(8,128)S(1)}, f32[8,64,128]{2,1,0:T(8,128)S(1)}, u32[]{:S(2)}, u32[]{:S(2)}) collective-permute-start(f32[8,64,128]{2,1,0:T(8,128)S(1)} %all_to_all.22.d_ref), channel_id=1, source_target_pairs={{0,32},{32,0},{64,96},{96,64},{128,160},{160,128},{192,224},{224,1... | collective-permute-start | bytes 786440 | tf_op jit(solution)/shard_map/ppermute | solution.py:438
  130.7 4.6 %collective-permute-start.6 = (f32[56,128]{1,0:T(8,128)S(1)}, f32[56,128]{1,0:T(8,128)S(1)}, u32[]{:S(2)}, u32[]{:S(2)}) collective-permute-start(f32[56,128]{1,0:T(8,128)S(1)} %get-tuple-element.32), channel_id=1, source_target_pairs={{0,1},{1,0},{2,3},{3,2},{4,5},{5,4},{6,7},{7,6},{8,9},{9,8},{10,11... | collective-permute-start | bytes 86024 | tf_op jit(solution)/shard_map/ppermute | solution.py:446
  136.1 12.5 %all-to-all-start.3 = ((f32[8,56,128]{2,1,0:T(8,128)}), f32[8,56,128]{2,1,0:T(8,128)S(1)}, u32[]{:S(2)}, u32[]{:S(2)}) async-start(f32[8,56,128]{2,1,0:T(8,128)} %broadcast_in_dim.5), calls=%async_computation.3 | async-start | bytes 458752 | tf_op jit(solution)/shard_map/all_to_all | solution.py:448

commit v4 on v3

--- a/solution.py
+++ b/solution.py
@@ -356,6 +356,22 @@
     for i in range(8):
         acc = acc + d_ref[i, :56, :] * slope[i : i + 1] + o_ref[i, :56, :] * slope[8 + i : 9 + i]
     out_ref[...] = acc
+
+
+def both_kernel(a_ref, b_ref, out_ref):
+    both = a_ref[...] + b_ref[...]
+    for i in range(8):
+        out_ref[i] = both
+
+
+def out_kernel(in_ref, down_ref, up_ref):
+    pad = jnp.zeros((384 - BW, 128), f32)
+    first = jnp.transpose(jnp.concatenate([in_ref[:BW], pad], axis=0))
+    low = in_ref[BW : BW + BW // 2]
+    low = jnp.transpose(jnp.concatenate([low, pltpu.roll(low, 64, 1), pad], axis=0))
+    down_ref[...] = first[:R, :BW]
+    up_ref[:64, :] = low[:64, :BW]
+    up_ref[64:, :] = first[R:, :BW]
 
 
 def on_device(hidden, lengths, starts, ranking, down_w, up_w, gain, head):
@@ -443,15 +459,23 @@
         out_specs=(VMEM, VMEM),
         compiler_params=pltpu.CompilerParams(vmem_limit_bytes=16 << 20),
     )(pieces, beside)
-    share = share + lax.ppermute(share, "prompt", [(0, 1), (1, 0)])
-    final = jnp.broadcast_to(share[None], (8, 56, 128))
+    final = pl.pallas_call(
+        both_kernel,
+        out_shape=jax.ShapeDtypeStruct((8, 56, 128), f32),
+        in_specs=[VMEM, VMEM],
+        out_specs=VMEM,
+        compiler_params=pltpu.CompilerParams(vmem_limit_bytes=16 << 20),
+    )(share, lax.ppermute(share, "prompt", [(0, 1), (1, 0)]))
     final = lax.all_to_all(final, "cand", 0, 0, axis_index_groups=along_z, tiled=True).reshape(448, 128)
+    down_grad, up_grad = pl.pallas_call(
+        out_kernel,
+        out_shape=(jax.ShapeDtypeStruct((R, BW), f32), jax.ShapeDtypeStruct((R, BW), f32)),
+        in_specs=[VMEM],
+        out_specs=(VMEM, VMEM),
+        compiler_params=pltpu.CompilerParams(vmem_limit_bytes=16 << 20),
+    )(final)
     half = BW + BW // 2
-    slab_a, slab_b = final[:BW], final[BW:half]
     pooled = final[half : half + 3].reshape(-1)[:BW]
-    down_grad = slab_a[:, :R].T
-    up_low = jnp.concatenate([slab_b[:, :64], slab_b[:, 64:]], axis=0)
-    up_grad = jnp.concatenate([up_low, slab_a[:, R:]], axis=1).T
     gain_f, head_f = gain.astype(f32), head.astype(f32)
     return (loss[0, :1], down_grad, up_grad, head_f * pooled, gain_f * pooled)
 

time: 154 us -> 153 us (level)
  local copies, waits for them, and re-layouts: 5.33 us -> 2.87 us
  Pallas kernels: 14.6 us -> 16.2 us
    pallas_call x0 -> x2, Pallas kernels: none -> 1.57 us  [the longest x1 0.86 us: on_device(): pl.pallas_call(out_kernel, out_shape=(jax.ShapeDtypeStruct((R, BW), f32),...]
    unnamed x12 -> x10, local copies, waits for them, and re-layouts: 3.92 us -> 2.35 us
where the time goes in v4:
time: 153 us; the launch traced here: 150 us
  blocking collectives  71.1 us (46%)
  waiting for transfers between devices  27.8 us (18%)
  starting transfers between devices  27.5 us (18%)
  Pallas kernels  16.2 us (11%)
  local copies, waits for them, and re-layouts  2.87 us (2%)
  other arithmetic  2.2 us (1%)
  between operations  2.11 us (1%)
    all_to_all x1, blocking collectives, on_device(): lax.all_to_all(coded_terms, 'fsdp', 0, 0, axis_index_groups=parity, tiled...  30.5 us
    all_to_all x1, blocking collectives, on_device(): lax.all_to_all(packed, 'fsdp', 0, 0, axis_index_groups=along_y, tiled=True)  21.3 us
    all_to_all x1, blocking collectives, on_device(): lax.all_to_all(sums, 'cand', 0, 0, axis_index_groups=along_z, tiled=True)  19.3 us
    ppermute x1, waiting for transfers between devices, on_device(): got_b = lax.ppermute(send_b, 'fsdp', turn)  12.5 us
    all_to_all x1, waiting for transfers between devices, on_device(): lax.all_to_all(final, 'cand', 0, 0, axis_index_groups=along_z, tiled=True)  8.57 us
    pallas_call x1, Pallas kernels, on_device(): pl.pallas_call(local_kernel, out_shape=(jax.ShapeDtypeStruct((8, CUT + 16...  7.37 us
    pallas_call x1, Pallas kernels, on_device(): pl.pallas_call(near_kernel, out_shape=(jax.ShapeDtypeStruct((HALF, 256),...  5.42 us
    ppermute x1, starting transfers between devices, on_device(): beside = lax.ppermute(pieces, 'cand', sibling)  5.24 us
  transfers between devices with their start and end apart: 8, of which 6 were waited for; matrix products, arithmetic and copies ran while one was open for 0% of the time, Pallas kernels for 4%

profile of v4, /device:TPU:1, one launch (start us, length us, event | category | flops | bytes accessed | tf_op | source)
XLA Modules:
  0.0 149.9 jit_solution(2852138131567126435)
XLA Ops:
  0.6 0.7 fusion
  1.3 0.9 broadcast_select_fusion
  2.3 0.2 shard_map.119
  2.5 21.3 %all_to_all.20.mine_ref = bf16[8,224,128]{2,1,0:T(8,128)(2,1)S(1)} all-to-all(bf16[8,224,128]{2,1,0:T(8,128)(2,1)S(1)} %shard_map.119), channel_id=1, replica_groups={{0,2,4,6,8,10,12,14},{16,18,20,22,24,26,28,30},{1,3,5,7,9,11,13,15},{17..., dimensions={0} | all-to-all | bytes 917504 | tf_op jit(solution)/shard_map/all_to_all | solution.py:394
  23.7 5.1 %collective-permute-start = (bf16[8,224,128]{2,1,0:T(8,128)(2,1)S(1)}, bf16[8,224,128]{2,1,0:T(8,128)(2,1)S(1)}, u32[]{:S(2)}, u32[]{:S(2)}) collective-permute-start(bf16[8,224,128]{2,1,0:T(8,128)(2,1)S(1)} %all_to_all.20.mine_ref), channel_id=1, source_target_pairs={{0,32},{32,0},{64,96},{96,64},{128,160},{160,128},{192,224},{224,1... | collective-permute-start | bytes 1376264 | tf_op jit(solution)/shard_map/ppermute | solution.py:397
  28.9 4.7 %collective-permute-start.1 = (bf16[8,224,128]{2,1,0:T(8,128)(2,1)S(1)}, bf16[8,224,128]{2,1,0:T(8,128)(2,1)S(1)}, u32[]{:S(2)}, u32[]{:S(2)}) collective-permute-start(bf16[8,224,128]{2,1,0:T(8,128)(2,1)S(1)} %all_to_all.20.mine_ref), channel_id=1, source_target_pairs={{0,16},{2,18},{4,20},{6,22},{8,24},{10,26},{12,28},{14,30},{16,0},... | collective-permute-start | bytes 1376264 | tf_op jit(solution)/shard_map/ppermute | solution.py:396
  33.5 0.0 copy-start
  33.6 2.3 %copy-done = bf16[1,1,512,4608]{3,2,1,0:T(8,128)(2,1)S(1)} copy-done((bf16[1,1,512,4608]{3,2,1,0:T(8,128)(2,1)S(1)}, bf16[1,1,512,4608]{3,2,1,0:T(8,128)(2,1)}, u32[]{:S(2)}) %copy-start) | copy-done | bytes 4718616
  35.9 5.4 %shard_map.120 = (bf16[2304,256]{1,0:T(8,128)(2,1)S(1)}, f32[512,256]{1,0:T(8,128)S(1)}, f32[256,256]{1,0:T(8,128)S(1)}, f32[512,128]{1,0:T(8,128)S(1)}) custom-call(bf16[512,4608]{1,0:T(8,128)(2,1)S(1)} %bitcast.5, bf16[8,224,128]{2,1,0:T(8,128)(2,1)S(1)} %all_to_all.20.mine_ref, bf16[8,224,128]{2,1,0:T(8,128)(2,1)S(1)} %collective-permute-done.other_ref), custom_call_target="tpu_custom_call" | custom-call | tf_op jit(solution)/shard_map/pallas_call | solution.py:398
  41.3 3.1 %collective-permute-done.1.mine_ref = bf16[8,224,128]{2,1,0:T(8,128)(2,1)S(1)} collective-permute-done((bf16[8,224,128]{2,1,0:T(8,128)(2,1)S(1)}, bf16[8,224,128]{2,1,0:T(8,128)(2,1)S(1)}, u32[]{:S(2)}, u32[]{:S(2)}) %collective-permute-start.1) | collective-permute-done | bytes 458784 | tf_op jit(solution)/shard_map/ppermute | solution.py:396
  44.4 2.7 %collective-permute-start.2 = (bf16[8,224,128]{2,1,0:T(8,128)(2,1)S(1)}, bf16[8,224,128]{2,1,0:T(8,128)(2,1)S(1)}, u32[]{:S(2)}, u32[]{:S(2)}) collective-permute-start(bf16[8,224,128]{2,1,0:T(8,128)(2,1)S(1)} %collective-permute-done.1.mine_ref), channel_id=1, source_target_pairs={{0,32},{32,0},{64,96},{96,64},{128,160},{160,128},{192,224},{224,1... | collective-permute-start | bytes 1376264 | tf_op jit(solution)/shard_map/ppermute | solution.py:411
  48.4 0.1 collective-permute-done.2.other_ref
  48.5 7.4 %shard_map.121 = (s16[8,240,128]{2,1,0:T(8,128)(2,1)S(1)}, s16[8,224,128]{2,1,0:T(8,128)(2,1)S(1)}, f32[8,288,128]{2,1,0:T(8,128)S(1)}, f32[8,144,128]{2,1,0:T(8...) custom-call(s32[1,1]{1,0:T(1,128)S(6)} %copy.14.starts, s32[1,1]{1,0:T(1,128)S(6)} %copy.13.lengths, ...), custom_call_target="tpu_custom_call" | custom-call | tf_op jit(solution)/shard_map/pallas_call | solution.py:413
  55.9 2.2 %collective-permute-start.3 = (s16[8,240,128]{2,1,0:T(8,128)(2,1)S(1)}, s16[8,240,128]{2,1,0:T(8,128)(2,1)S(1)}, u32[]{:S(2)}, u32[]{:S(2)}) collective-permute-start(s16[8,240,128]{2,1,0:T(8,128)(2,1)S(1)} %get-tuple-element.27), channel_id=1, source_target_pairs={{0,2},{2,0},{4,6},{6,4},{8,10},{10,8},{12,14},{14,12},{16,18},{18,... | collective-permute-start | bytes 1474568 | tf_op jit(solution)/shard_map/ppermute | solution.py:433
  58.1 2.0 %collective-permute-start.4 = (s16[8,224,128]{2,1,0:T(8,128)(2,1)S(1)}, s16[8,224,128]{2,1,0:T(8,128)(2,1)S(1)}, u32[]{:S(2)}, u32[]{:S(2)}) collective-permute-start(s16[8,224,128]{2,1,0:T(8,128)(2,1)S(1)} %get-tuple-element.28), channel_id=1, source_target_pairs={{0,14},{2,4},{4,2},{6,8},{8,6},{10,12},{12,10},{14,0},{16,30},{18,... | collective-permute-start | bytes 1376264 | tf_op jit(solution)/shard_map/ppermute | solution.py:435
  60.1 12.5 %collective-permute-done.4.got_b = s16[8,224,128]{2,1,0:T(8,128)(2,1)S(1)} collective-permute-done((s16[8,224,128]{2,1,0:T(8,128)(2,1)S(1)}, s16[8,224,128]{2,1,0:T(8,128)(2,1)S(1)}, u32[]{:S(2)}, u32[]{:S(2)}) %collective-permute-start.4) | collective-permute-done | bytes 458784 | tf_op jit(solution)/shard_map/ppermute | solution.py:435
  72.6 0.6 shard_map.122
  73.3 0.0 copy-start.2
  73.3 30.5 %all_to_all.21.q_ref = s16[8,448,128]{2,1,0:T(8,128)(2,1)S(1)} all-to-all(s16[8,448,128]{2,1,0:T(8,128)(2,1)S(1)} %shard_map.122), channel_id=1, replica_groups={{0,4,8,12,16,20,24,28},{2,6,10,14,18,22,26,30},{1,5,9,13,17,21,25,29},{..., dimensions={0} | all-to-all | bytes 1835008 | tf_op jit(solution)/shard_map/all_to_all | solution.py:444
  103.8 0.8 shard_map.123
  104.6 19.3 %all_to_all.22.d_ref = f32[8,64,128]{2,1,0:T(8,128)S(1)} all-to-all(f32[8,64,128]{2,1,0:T(8,128)S(1)} %shard_map.123), channel_id=1, replica_groups={{0,64,128,192,256,320,384,448},{32,96,160,224,288,352,416,480},{1,65,12..., dimensions={0} | all-to-all | bytes 524288 | tf_op jit(solution)/shard_map/all_to_all | solution.py:453
  124.0 5.2 %collective-permute-start.5 = (f32[8,64,128]{2,1,0:T(8,128)S(1)}, f32[8,64,128]{2,1,0:T(8,128)S(1)}, u32[]{:S(2)}, u32[]{:S(2)}) collective-permute-start(f32[8,64,128]{2,1,0:T(8,128)S(1)} %all_to_all.22.d_ref), channel_id=1, source_target_pairs={{0,32},{32,0},{64,96},{96,64},{128,160},{160,128},{192,224},{224,1... | collective-permute-start | bytes 786440 | tf_op jit(solution)/shard_map/ppermute | solution.py:454
  129.2 1.1 collective-permute-done.5.o_ref
  130.4 0.2 shard_map.124
  130.6 2.2 %collective-permute-start.6 = (f32[56,128]{1,0:T(8,128)S(1)}, f32[56,128]{1,0:T(8,128)S(1)}, u32[]{:S(2)}, u32[]{:S(2)}) collective-permute-start(f32[56,128]{1,0:T(8,128)S(1)} %get-tuple-element.34.a_ref), channel_id=1, source_target_pairs={{0,1},{1,0},{2,3},{3,2},{4,5},{5,4},{6,7},{7,6},{8,9},{9,8},{10,11... | collective-permute-start | bytes 86024 | tf_op jit(solution)/shard_map/ppermute | solution.py:468
  132.9 2.4 %collective-permute-done.6.b_ref = f32[56,128]{1,0:T(8,128)S(1)} collective-permute-done((f32[56,128]{1,0:T(8,128)S(1)}, f32[56,128]{1,0:T(8,128)S(1)}, u32[]{:S(2)}, u32[]{:S(2)}) %collective-permute-start.6) | collective-permute-done | bytes 28704 | tf_op jit(solution)/shard_map/ppermute | solution.py:468
  135.2 0.7 shard_map.125
  135.9 3.4 %all-to-all-start.3 = ((f32[8,56,128]{2,1,0:T(8,128)}), f32[8,56,128]{2,1,0:T(8,128)S(1)}, u32[]{:S(2)}, u32[]{:S(2)}) async-start(f32[8,56,128]{2,1,0:T(8,128)} %shard_map.125), calls=%async_computation.3 | async-start | bytes 458752 | tf_op jit(solution)/shard_map/all_to_all | solution.py:469
  139.3 0.5 slice.9
  139.9 8.6 %all-to-all-done.3 = f32[8,56,128]{2,1,0:T(8,128)S(1)} async-done(((f32[8,56,128]{2,1,0:T(8,128)}), f32[8,56,128]{2,1,0:T(8,128)S(1)}, u32[]{:S(2)}, u32[]{:S(2)}) %all-to-all-start.3) | async-done | bytes 229408 | tf_op jit(solution)/shard_map/all_to_all | solution.py:469
  148.4 0.9 shard_map.126
  149.3 0.6 convert_multiply_fusion.2
  (12 shorter events, 0.0 us)
Async XLA Ops:
  23.7 9.8 %collective-permute-start = (bf16[8,224,128]{2,1,0:T(8,128)(2,1)S(1)}, bf16[8,224,128]{2,1,0:T(8,128)(2,1)S(1)}, u32[]{:S(2)}, u32[]{:S(2)}) collective-permute-start(bf16[8,224,128]{2,1,0:T(8,128)(2,1)S(1)} %all_to_all.20.mine_ref), channel_id=1, source_target_pairs={{0,32},{32,0},{64,96},{96,64},{128,160},{160,128},{192,224},{224,1... | collective-permute-start | bytes 1376264 | tf_op jit(solution)/shard_map/ppermute | solution.py:397
  28.9 15.5 %collective-permute-start.1 = (bf16[8,224,128]{2,1,0:T(8,128)(2,1)S(1)}, bf16[8,224,128]{2,1,0:T(8,128)(2,1)S(1)}, u32[]{:S(2)}, u32[]{:S(2)}) collective-permute-start(bf16[8,224,128]{2,1,0:T(8,128)(2,1)S(1)} %all_to_all.20.mine_ref), channel_id=1, source_target_pairs={{0,16},{2,18},{4,20},{6,22},{8,24},{10,26},{12,28},{14,30},{16,0},... | collective-permute-start | bytes 1376264 | tf_op jit(solution)/shard_map/ppermute | solution.py:396
  33.5 2.3 %copy-start = (bf16[1,1,512,4608]{3,2,1,0:T(8,128)(2,1)S(1)}, bf16[1,1,512,4608]{3,2,1,0:T(8,128)(2,1)}, u32[]{:S(2)}) copy-start(bf16[1,1,512,4608]{3,2,1,0:T(8,128)(2,1)} %param.8) | copy-start | bytes 14155780
  35.9 12.7 %copy-start.1 = (bf16[1,1,512,4608]{3,2,1,0:T(8,128)(2,1)S(1)}, bf16[1,1,512,4608]{3,2,1,0:T(8,128)(2,1)}, u32[]{:S(2)}) copy-start(bf16[1,1,512,4608]{3,2,1,0:T(8,128)(2,1)} %param.8) | copy-start | bytes 14155780
  44.4 4.1 %collective-permute-start.2 = (bf16[8,224,128]{2,1,0:T(8,128)(2,1)S(1)}, bf16[8,224,128]{2,1,0:T(8,128)(2,1)S(1)}, u32[]{:S(2)}, u32[]{:S(2)}) collective-permute-start(bf16[8,224,128]{2,1,0:T(8,128)(2,1)S(1)} %collective-permute-done.1.mine_ref), channel_id=1, source_target_pairs={{0,32},{32,0},{64,96},{96,64},{128,160},{160,128},{192,224},{224,1... | collective-permute-start | bytes 1376264 | tf_op jit(solution)/shard_map/ppermute | solution.py:411
  55.9 16.7 %collective-permute-start.3 = (s16[8,240,128]{2,1,0:T(8,128)(2,1)S(1)}, s16[8,240,128]{2,1,0:T(8,128)(2,1)S(1)}, u32[]{:S(2)}, u32[]{:S(2)}) collective-permute-start(s16[8,240,128]{2,1,0:T(8,128)(2,1)S(1)} %get-tuple-element.27), channel_id=1, source_target_pairs={{0,2},{2,0},{4,6},{6,4},{8,10},{10,8},{12,14},{14,12},{16,18},{18,... | collective-permute-start | bytes 1474568 | tf_op jit(solution)/shard_map/ppermute | solution.py:433
  58.1 14.5 %collective-permute-start.4 = (s16[8,224,128]{2,1,0:T(8,128)(2,1)S(1)}, s16[8,224,128]{2,1,0:T(8,128)(2,1)S(1)}, u32[]{:S(2)}, u32[]{:S(2)}) collective-permute-start(s16[8,224,128]{2,1,0:T(8,128)(2,1)S(1)} %get-tuple-element.28), channel_id=1, source_target_pairs={{0,14},{2,4},{4,2},{6,8},{8,6},{10,12},{12,10},{14,0},{16,30},{18,... | collective-permute-start | bytes 1376264 | tf_op jit(solution)/shard_map/ppermute | solution.py:435
  73.3 30.5 %copy-start.2 = (s32[1,16]{1,0:T(1,128)S(1)}, s32[1,16]{1,0:T(1,128)}, u32[]{:S(2)}) copy-start(s32[1,16]{1,0:T(1,128)} %ranking.1) | copy-start | bytes 196
  104.6 44.7 %copy-start.3 = (bf16[288]{0:T(512)(128)(2,1)S(1)}, bf16[288]{0:T(512)(128)(2,1)}, u32[]{:S(2)}) copy-start(bf16[288]{0:T(512)(128)(2,1)} %param.15) | copy-start | bytes 1732
  104.6 44.7 %copy-start.4 = (bf16[288]{0:T(512)(128)(2,1)S(1)}, bf16[288]{0:T(512)(128)(2,1)}, u32[]{:S(2)}) copy-start(bf16[288]{0:T(512)(128)(2,1)} %param.14) | copy-start | bytes 1732
  124.0 6.4 %collective-permute-start.5 = (f32[8,64,128]{2,1,0:T(8,128)S(1)}, f32[8,64,128]{2,1,0:T(8,128)S(1)}, u32[]{:S(2)}, u32[]{:S(2)}) collective-permute-start(f32[8,64,128]{2,1,0:T(8,128)S(1)} %all_to_all.22.d_ref), channel_id=1, source_target_pairs={{0,32},{32,0},{64,96},{96,64},{128,160},{160,128},{192,224},{224,1... | collective-permute-start | bytes 786440 | tf_op jit(solution)/shard_map/ppermute | solution.py:454
  130.6 4.6 %collective-permute-start.6 = (f32[56,128]{1,0:T(8,128)S(1)}, f32[56,128]{1,0:T(8,128)S(1)}, u32[]{:S(2)}, u32[]{:S(2)}) collective-permute-start(f32[56,128]{1,0:T(8,128)S(1)} %get-tuple-element.34.a_ref), channel_id=1, source_target_pairs={{0,1},{1,0},{2,3},{3,2},{4,5},{5,4},{6,7},{7,6},{8,9},{9,8},{10,11... | collective-permute-start | bytes 86024 | tf_op jit(solution)/shard_map/ppermute | solution.py:468
  135.9 12.5 %all-to-all-start.3 = ((f32[8,56,128]{2,1,0:T(8,128)}), f32[8,56,128]{2,1,0:T(8,128)S(1)}, u32[]{:S(2)}, u32[]{:S(2)}) async-start(f32[8,56,128]{2,1,0:T(8,128)} %shard_map.125), calls=%async_computation.3 | async-start | bytes 458752 | tf_op jit(solution)/shard_map/all_to_all | solution.py:469

commit v5 on v4

--- a/solution.py
+++ b/solution.py
@@ -135,7 +135,7 @@
             unpack(other_ref, second)
 
 
-def near_kernel(x_ref, mine_ref, other_ref, w_ref, prod_ref, gram_ref, ss_ref):
+def near_kernel(x_ref, mine_ref, other_ref, w_ref, prod_ref, gram_ref, ss_ref, t_ref):
     unpack_both(lax.axis_index("cand") % 2, mine_ref, other_ref, w_ref)
 
     def square(i, carry):
@@ -147,6 +147,9 @@
     lax.fori_loop(0, TOK // 16, square, 0)
     cols = pl.ds(pl.multiple_of(lax.axis_index("fsdp") // 8 * HALF, 128), HALF)
     prod_ref[...] = mm(x_ref[:, cols], w_ref[...], 1, 0)
+    for i in range(D // CH):
+        cut = slice(i * CH, (i + 1) * CH)
+        t_ref[cut, :] = jnp.transpose(x_ref[:, cut])
     gram_ref[...] = mm(w_ref[...], w_ref[...], 0, 0)
 
 
@@ -158,6 +161,7 @@
     prod_near,
     gram_near,
     ss_ref,
+    t_ref,
     mine_ref,
     other_ref,
     send_a,
@@ -223,7 +227,7 @@
     for i in range(D // CH):
         cut = slice(i * CH, (i + 1) * CH)
         w = w_ref[cut, :]
-        g_ref[cut, :] = mm(x_ref[:, cut], lhs, 0, 0) + (mm(w, c_hi, 1, 0) + mm(w, c_lo, 1, 0))
+        g_ref[cut, :] = mm(t_ref[cut, :], lhs, 1, 0) + (mm(w, c_hi, 1, 0) + mm(w, c_lo, 1, 0))
 
     al_hi = alpha.astype(bf16).astype(f32)
     al_lo = alpha - al_hi
@@ -395,16 +399,17 @@
     across = [(i, i ^ 8) for i in range(16)]
     far_mine = lax.ppermute(mine, "fsdp", across)
     other = lax.ppermute(mine, "cand", sibling)
-    w_near, prod, gram, squares = pl.pallas_call(
+    w_near, prod, gram, squares, x_t = pl.pallas_call(
         near_kernel,
         out_shape=(
             jax.ShapeDtypeStruct((HALF, 256), bf16),
             jax.ShapeDtypeStruct((TOK, 256), f32),
             jax.ShapeDtypeStruct((256, 256), f32),
             jax.ShapeDtypeStruct((TOK, 128), f32),
+            jax.ShapeDtypeStruct((D, TOK), bf16),
         ),
         in_specs=[VMEM, VMEM, VMEM],
-        out_specs=(VMEM, VMEM, VMEM, VMEM),
+        out_specs=(VMEM, VMEM, VMEM, VMEM, VMEM),
         compiler_params=pltpu.CompilerParams(vmem_limit_bytes=24 << 20),
     )(x, mine, other)
     far_mine, squares = lax.optimization_barrier((far_mine, squares))
@@ -420,7 +425,7 @@
             jax.ShapeDtypeStruct((8, 8, 512), f32),
             jax.ShapeDtypeStruct((8, 128), f32),
         ),
-        in_specs=[SMEM, SMEM] + [VMEM] * 7,
+        in_specs=[SMEM, SMEM] + [VMEM] * 8,
         out_specs=(VMEM,) * 6,
         scratch_shapes=[
             pltpu.VMEM((HALF, 256), bf16),
@@ -429,7 +434,7 @@
             pltpu.VMEM((8, D + 256), f32),
         ],
         compiler_params=pltpu.CompilerParams(vmem_limit_bytes=40 << 20),
-    )(starts, lengths, x, w_near, prod, gram, squares, far_mine, far_other)
+    )(starts, lengths, x, w_near, prod, gram, squares, x_t, far_mine, far_other)
     got_a = lax.ppermute(send_a, "fsdp", [(i, i ^ 1) for i in range(16)])
     turn = [(i, i // 8 * 8 + (i + (1 if i % 2 else 7)) % 8) for i in range(16)]
     got_b = lax.ppermute(send_b, "fsdp", turn)

time: 153 us -> 155 us (1.013)
  Pallas kernels: 16.2 us -> 18.9 us
  waiting for transfers between devices: 27.8 us -> 25.2 us
  local copies, waits for them, and re-layouts: 2.87 us -> 4.99 us
    ppermute x1, waiting for transfers between devices: 3.1 us -> 0.47 us  [on_device(): far_mine = lax.ppermute(mine, 'fsdp', across)]
    pallas_call x1, Pallas kernels: 7.37 us -> 9.6 us  [on_device(): pl.pallas_call(local_kernel, out_shape=(jax.ShapeDtypeStruct((8, CUT + 16...]
    unnamed x10 -> x12, local copies, waits for them, and re-layouts: 2.35 us -> 4.47 us
where the time goes in v5:
time: 155 us; the launch traced here: 152 us
  blocking collectives  71.1 us (46%)
  starting transfers between devices  27.6 us (18%)
  waiting for transfers between devices  25.2 us (16%)
  Pallas kernels  18.9 us (12%)
  local copies, waits for them, and re-layouts  4.99 us (3%)
  other arithmetic  2.2 us (1%)
  between operations  2.12 us (1%)
    all_to_all x1, blocking collectives, on_device(): lax.all_to_all(coded_terms, 'fsdp', 0, 0, axis_index_groups=parity, tiled...  30.5 us
    all_to_all x1, blocking collectives, on_device(): lax.all_to_all(packed, 'fsdp', 0, 0, axis_index_groups=along_y, tiled=True)  21.3 us
    all_to_all x1, blocking collectives, on_device(): lax.all_to_all(sums, 'cand', 0, 0, axis_index_groups=along_z, tiled=True)  19.3 us
    ppermute x1, waiting for transfers between devices, on_device(): got_b = lax.ppermute(send_b, 'fsdp', turn)  12.5 us
    pallas_call x1, Pallas kernels, on_device(): pl.pallas_call(local_kernel, out_shape=(jax.ShapeDtypeStruct((8, CUT + 16...  9.6 us
    all_to_all x1, waiting for transfers between devices, on_device(): lax.all_to_all(final, 'cand', 0, 0, axis_index_groups=along_z, tiled=True)  8.57 us
    pallas_call x1, Pallas kernels, on_device(): pl.pallas_call(near_kernel, out_shape=(jax.ShapeDtypeStruct((HALF, 256),...  5.92 us
    ppermute x1, starting transfers between devices, on_device(): beside = lax.ppermute(pieces, 'cand', sibling)  5.25 us
  transfers between devices with their start and end apart: 8, of which 6 were waited for; matrix products, arithmetic and copies ran while one was open for 0% of the time, Pallas kernels for 4%

profile of v5, /device:TPU:1, one launch (start us, length us, event | category | flops | bytes accessed | tf_op | source)
XLA Modules:
  0.0 152.2 jit_solution(11413152808745289699)
XLA Ops:
  0.6 0.7 fusion
  1.3 0.9 broadcast_select_fusion
  2.3 0.2 shard_map.119
  2.5 21.3 %all_to_all.20.mine_ref = bf16[8,224,128]{2,1,0:T(8,128)(2,1)S(1)} all-to-all(bf16[8,224,128]{2,1,0:T(8,128)(2,1)S(1)} %shard_map.119), channel_id=1, replica_groups={{0,2,4,6,8,10,12,14},{16,18,20,22,24,26,28,30},{1,3,5,7,9,11,13,15},{17..., dimensions={0} | all-to-all | bytes 917504 | tf_op jit(solution)/shard_map/all_to_all | solution.py:398
  23.7 5.1 %collective-permute-start = (bf16[8,224,128]{2,1,0:T(8,128)(2,1)S(1)}, bf16[8,224,128]{2,1,0:T(8,128)(2,1)S(1)}, u32[]{:S(2)}, u32[]{:S(2)}) collective-permute-start(bf16[8,224,128]{2,1,0:T(8,128)(2,1)S(1)} %all_to_all.20.mine_ref), channel_id=1, source_target_pairs={{0,32},{32,0},{64,96},{96,64},{128,160},{160,128},{192,224},{224,1... | collective-permute-start | bytes 1376264 | tf_op jit(solution)/shard_map/ppermute | solution.py:401
  28.9 4.7 %collective-permute-start.1 = (bf16[8,224,128]{2,1,0:T(8,128)(2,1)S(1)}, bf16[8,224,128]{2,1,0:T(8,128)(2,1)S(1)}, u32[]{:S(2)}, u32[]{:S(2)}) collective-permute-start(bf16[8,224,128]{2,1,0:T(8,128)(2,1)S(1)} %all_to_all.20.mine_ref), channel_id=1, source_target_pairs={{0,16},{2,18},{4,20},{6,22},{8,24},{10,26},{12,28},{14,30},{16,0},... | collective-permute-start | bytes 1376264 | tf_op jit(solution)/shard_map/ppermute | solution.py:400
  33.6 2.3 %copy-done = bf16[1,1,512,4608]{3,2,1,0:T(8,128)(2,1)S(1)} copy-done((bf16[1,1,512,4608]{3,2,1,0:T(8,128)(2,1)S(1)}, bf16[1,1,512,4608]{3,2,1,0:T(8,128)(2,1)}, u32[]{:S(2)}) %copy-start) | copy-done | bytes 4718616
  35.9 5.9 %shard_map.120 = (bf16[2304,256]{1,0:T(8,128)(2,1)S(1)}, f32[512,256]{1,0:T(8,128)S(1)}, f32[256,256]{1,0:T(8,128)S(1)}, f32[512,128]{1,0:T(8,128)S(1)}, bf16[4608,512]{1,0:T(8,128)(2,1)S(1)}) custom-call(bf16[512,4608]{1,0:T(8,128)(2,1)S(1)} %bitcast.5, bf16[8,224,128]{2,1,0:T(8,128)(2,1)S(1)} %all_to_all.20.mine_ref, ...), custom_call_target="tpu_custom_call" | custom-call | tf_op jit(solution)/shard_map/pallas_call | solution.py:402
  41.8 2.1 %copy-done.2 = bf16[4608,512]{1,0:T(8,128)(2,1)} copy-done((bf16[4608,512]{1,0:T(8,128)(2,1)}, bf16[4608,512]{1,0:T(8,128)(2,1)S(1)}, u32[]{:S(2)}) %copy-start.2) | copy-done | bytes 4718616
  43.9 0.5 collective-permute-done.1.mine_ref
  44.4 2.7 %collective-permute-start.2 = (bf16[8,224,128]{2,1,0:T(8,128)(2,1)S(1)}, bf16[8,224,128]{2,1,0:T(8,128)(2,1)S(1)}, u32[]{:S(2)}, u32[]{:S(2)}) collective-permute-start(bf16[8,224,128]{2,1,0:T(8,128)(2,1)S(1)} %collective-permute-done.1.mine_ref), channel_id=1, source_target_pairs={{0,32},{32,0},{64,96},{96,64},{128,160},{160,128},{192,224},{224,1... | collective-permute-start | bytes 1376264 | tf_op jit(solution)/shard_map/ppermute | solution.py:416
  48.4 0.1 collective-permute-done.2.other_ref
  48.5 9.6 %shard_map.121 = (s16[8,240,128]{2,1,0:T(8,128)(2,1)S(1)}, s16[8,224,128]{2,1,0:T(8,128)(2,1)S(1)}, f32[8,288,128]{2,1,0:T(8,128)S(1)}, f32[8,144,128]{2,1,0:T(8...) custom-call(s32[1,1]{1,0:T(1,128)S(6)} %copy.14.starts, s32[1,1]{1,0:T(1,128)S(6)} %copy.13.lengths, ...), custom_call_target="tpu_custom_call" | custom-call | tf_op jit(solution)/shard_map/pallas_call | solution.py:418
  58.2 0.0 copy-start.5
  58.2 2.3 %collective-permute-start.3 = (s16[8,240,128]{2,1,0:T(8,128)(2,1)S(1)}, s16[8,240,128]{2,1,0:T(8,128)(2,1)S(1)}, u32[]{:S(2)}, u32[]{:S(2)}) collective-permute-start(s16[8,240,128]{2,1,0:T(8,128)(2,1)S(1)} %get-tuple-element.29), channel_id=1, source_target_pairs={{0,2},{2,0},{4,6},{6,4},{8,10},{10,8},{12,14},{14,12},{16,18},{18,... | collective-permute-start | bytes 1474568 | tf_op jit(solution)/shard_map/ppermute | solution.py:438
  60.5 2.0 %collective-permute-start.4 = (s16[8,224,128]{2,1,0:T(8,128)(2,1)S(1)}, s16[8,224,128]{2,1,0:T(8,128)(2,1)S(1)}, u32[]{:S(2)}, u32[]{:S(2)}) collective-permute-start(s16[8,224,128]{2,1,0:T(8,128)(2,1)S(1)} %get-tuple-element.30), channel_id=1, source_target_pairs={{0,14},{2,4},{4,2},{6,8},{8,6},{10,12},{12,10},{14,0},{16,30},{18,... | collective-permute-start | bytes 1376264 | tf_op jit(solution)/shard_map/ppermute | solution.py:440
  62.5 12.5 %collective-permute-done.4.got_b = s16[8,224,128]{2,1,0:T(8,128)(2,1)S(1)} collective-permute-done((s16[8,224,128]{2,1,0:T(8,128)(2,1)S(1)}, s16[8,224,128]{2,1,0:T(8,128)(2,1)S(1)}, u32[]{:S(2)}, u32[]{:S(2)}) %collective-permute-start.4) | collective-permute-done | bytes 458784 | tf_op jit(solution)/shard_map/ppermute | solution.py:440
  75.0 0.6 shard_map.122
  75.7 30.5 %all_to_all.21.q_ref = s16[8,448,128]{2,1,0:T(8,128)(2,1)S(1)} all-to-all(s16[8,448,128]{2,1,0:T(8,128)(2,1)S(1)} %shard_map.122), channel_id=1, replica_groups={{0,4,8,12,16,20,24,28},{2,6,10,14,18,22,26,30},{1,5,9,13,17,21,25,29},{..., dimensions={0} | all-to-all | bytes 1835008 | tf_op jit(solution)/shard_map/all_to_all | solution.py:449
  106.2 0.8 shard_map.123
  107.0 19.3 %all_to_all.22.d_ref = f32[8,64,128]{2,1,0:T(8,128)S(1)} all-to-all(f32[8,64,128]{2,1,0:T(8,128)S(1)} %shard_map.123), channel_id=1, replica_groups={{0,64,128,192,256,320,384,448},{32,96,160,224,288,352,416,480},{1,65,12..., dimensions={0} | all-to-all | bytes 524288 | tf_op jit(solution)/shard_map/all_to_all | solution.py:458
  126.3 5.2 %collective-permute-start.5 = (f32[8,64,128]{2,1,0:T(8,128)S(1)}, f32[8,64,128]{2,1,0:T(8,128)S(1)}, u32[]{:S(2)}, u32[]{:S(2)}) collective-permute-start(f32[8,64,128]{2,1,0:T(8,128)S(1)} %all_to_all.22.d_ref), channel_id=1, source_target_pairs={{0,32},{32,0},{64,96},{96,64},{128,160},{160,128},{192,224},{224,1... | collective-permute-start | bytes 786440 | tf_op jit(solution)/shard_map/ppermute | solution.py:459
  131.6 1.1 collective-permute-done.5.o_ref
  132.7 0.2 shard_map.124
  133.0 2.2 %collective-permute-start.6 = (f32[56,128]{1,0:T(8,128)S(1)}, f32[56,128]{1,0:T(8,128)S(1)}, u32[]{:S(2)}, u32[]{:S(2)}) collective-permute-start(f32[56,128]{1,0:T(8,128)S(1)} %get-tuple-element.36.a_ref), channel_id=1, source_target_pairs={{0,1},{1,0},{2,3},{3,2},{4,5},{5,4},{6,7},{7,6},{8,9},{9,8},{10,11... | collective-permute-start | bytes 86024 | tf_op jit(solution)/shard_map/ppermute | solution.py:473
  135.2 2.4 %collective-permute-done.6.b_ref = f32[56,128]{1,0:T(8,128)S(1)} collective-permute-done((f32[56,128]{1,0:T(8,128)S(1)}, f32[56,128]{1,0:T(8,128)S(1)}, u32[]{:S(2)}, u32[]{:S(2)}) %collective-permute-start.6) | collective-permute-done | bytes 28704 | tf_op jit(solution)/shard_map/ppermute | solution.py:473
  137.6 0.7 shard_map.125
  138.3 3.4 %all-to-all-start.3 = ((f32[8,56,128]{2,1,0:T(8,128)}), f32[8,56,128]{2,1,0:T(8,128)S(1)}, u32[]{:S(2)}, u32[]{:S(2)}) async-start(f32[8,56,128]{2,1,0:T(8,128)} %shard_map.125), calls=%async_computation.3 | async-start | bytes 458752 | tf_op jit(solution)/shard_map/all_to_all | solution.py:474
  141.7 0.5 slice.9
  142.2 8.6 %all-to-all-done.3 = f32[8,56,128]{2,1,0:T(8,128)S(1)} async-done(((f32[8,56,128]{2,1,0:T(8,128)}), f32[8,56,128]{2,1,0:T(8,128)S(1)}, u32[]{:S(2)}, u32[]{:S(2)}) %all-to-all-start.3) | async-done | bytes 229408 | tf_op jit(solution)/shard_map/all_to_all | solution.py:474
  150.8 0.9 shard_map.126
  151.6 0.6 convert_multiply_fusion.2
  (14 shorter events, 0.1 us)
Async XLA Ops:
  23.7 9.8 %collective-permute-start = (bf16[8,224,128]{2,1,0:T(8,128)(2,1)S(1)}, bf16[8,224,128]{2,1,0:T(8,128)(2,1)S(1)}, u32[]{:S(2)}, u32[]{:S(2)}) collective-permute-start(bf16[8,224,128]{2,1,0:T(8,128)(2,1)S(1)} %all_to_all.20.mine_ref), channel_id=1, source_target_pairs={{0,32},{32,0},{64,96},{96,64},{128,160},{160,128},{192,224},{224,1... | collective-permute-start | bytes 1376264 | tf_op jit(solution)/shard_map/ppermute | solution.py:401
  28.9 15.5 %collective-permute-start.1 = (bf16[8,224,128]{2,1,0:T(8,128)(2,1)S(1)}, bf16[8,224,128]{2,1,0:T(8,128)(2,1)S(1)}, u32[]{:S(2)}, u32[]{:S(2)}) collective-permute-start(bf16[8,224,128]{2,1,0:T(8,128)(2,1)S(1)} %all_to_all.20.mine_ref), channel_id=1, source_target_pairs={{0,16},{2,18},{4,20},{6,22},{8,24},{10,26},{12,28},{14,30},{16,0},... | collective-permute-start | bytes 1376264 | tf_op jit(solution)/shard_map/ppermute | solution.py:400
  33.5 2.3 %copy-start = (bf16[1,1,512,4608]{3,2,1,0:T(8,128)(2,1)S(1)}, bf16[1,1,512,4608]{3,2,1,0:T(8,128)(2,1)}, u32[]{:S(2)}) copy-start(bf16[1,1,512,4608]{3,2,1,0:T(8,128)(2,1)} %param.8) | copy-start | bytes 14155780
  35.9 12.7 %copy-start.1 = (bf16[1,1,512,4608]{3,2,1,0:T(8,128)(2,1)S(1)}, bf16[1,1,512,4608]{3,2,1,0:T(8,128)(2,1)}, u32[]{:S(2)}) copy-start(bf16[1,1,512,4608]{3,2,1,0:T(8,128)(2,1)} %param.8) | copy-start | bytes 14155780
  41.8 2.1 %copy-start.2 = (bf16[4608,512]{1,0:T(8,128)(2,1)}, bf16[4608,512]{1,0:T(8,128)(2,1)S(1)}, u32[]{:S(2)}) copy-start(bf16[4608,512]{1,0:T(8,128)(2,1)S(1)} %get-tuple-element.27.t_ref) | copy-start | bytes 14155780
  44.4 4.1 %collective-permute-start.2 = (bf16[8,224,128]{2,1,0:T(8,128)(2,1)S(1)}, bf16[8,224,128]{2,1,0:T(8,128)(2,1)S(1)}, u32[]{:S(2)}, u32[]{:S(2)}) collective-permute-start(bf16[8,224,128]{2,1,0:T(8,128)(2,1)S(1)} %collective-permute-done.1.mine_ref), channel_id=1, source_target_pairs={{0,32},{32,0},{64,96},{96,64},{128,160},{160,128},{192,224},{224,1... | collective-permute-start | bytes 1376264 | tf_op jit(solution)/shard_map/ppermute | solution.py:416
  58.1 48.0 %copy-start.3 = (s32[1,16]{1,0:T(1,128)S(1)}, s32[1,16]{1,0:T(1,128)}, u32[]{:S(2)}) copy-start(s32[1,16]{1,0:T(1,128)} %ranking.1) | copy-start | bytes 196
  58.2 93.5 %copy-start.4 = (bf16[288]{0:T(512)(128)(2,1)S(1)}, bf16[288]{0:T(512)(128)(2,1)}, u32[]{:S(2)}) copy-start(bf16[288]{0:T(512)(128)(2,1)} %param.15) | copy-start | bytes 1732
  58.2 93.4 %copy-start.5 = (bf16[288]{0:T(512)(128)(2,1)S(1)}, bf16[288]{0:T(512)(128)(2,1)}, u32[]{:S(2)}) copy-start(bf16[288]{0:T(512)(128)(2,1)} %param.14) | copy-start | bytes 1732
  58.2 16.8 %collective-permute-start.3 = (s16[8,240,128]{2,1,0:T(8,128)(2,1)S(1)}, s16[8,240,128]{2,1,0:T(8,128)(2,1)S(1)}, u32[]{:S(2)}, u32[]{:S(2)}) collective-permute-start(s16[8,240,128]{2,1,0:T(8,128)(2,1)S(1)} %get-tuple-element.29), channel_id=1, source_target_pairs={{0,2},{2,0},{4,6},{6,4},{8,10},{10,8},{12,14},{14,12},{16,18},{18,... | collective-permute-start | bytes 1474568 | tf_op jit(solution)/shard_map/ppermute | solution.py:438
  60.5 14.5 %collective-permute-start.4 = (s16[8,224,128]{2,1,0:T(8,128)(2,1)S(1)}, s16[8,224,128]{2,1,0:T(8,128)(2,1)S(1)}, u32[]{:S(2)}, u32[]{:S(2)}) collective-permute-start(s16[8,224,128]{2,1,0:T(8,128)(2,1)S(1)} %get-tuple-element.30), channel_id=1, source_target_pairs={{0,14},{2,4},{4,2},{6,8},{8,6},{10,12},{12,10},{14,0},{16,30},{18,... | collective-permute-start | bytes 1376264 | tf_op jit(solution)/shard_map/ppermute | solution.py:440
  126.3 6.4 %collective-permute-start.5 = (f32[8,64,128]{2,1,0:T(8,128)S(1)}, f32[8,64,128]{2,1,0:T(8,128)S(1)}, u32[]{:S(2)}, u32[]{:S(2)}) collective-permute-start(f32[8,64,128]{2,1,0:T(8,128)S(1)} %all_to_all.22.d_ref), channel_id=1, source_target_pairs={{0,32},{32,0},{64,96},{96,64},{128,160},{160,128},{192,224},{224,1... | collective-permute-start | bytes 786440 | tf_op jit(solution)/shard_map/ppermute | solution.py:459
  133.0 4.6 %collective-permute-start.6 = (f32[56,128]{1,0:T(8,128)S(1)}, f32[56,128]{1,0:T(8,128)S(1)}, u32[]{:S(2)}, u32[]{:S(2)}) collective-permute-start(f32[56,128]{1,0:T(8,128)S(1)} %get-tuple-element.36.a_ref), channel_id=1, source_target_pairs={{0,1},{1,0},{2,3},{3,2},{4,5},{5,4},{6,7},{7,6},{8,9},{9,8},{10,11... | collective-permute-start | bytes 86024 | tf_op jit(solution)/shard_map/ppermute | solution.py:473
  138.3 12.5 %all-to-all-start.3 = ((f32[8,56,128]{2,1,0:T(8,128)}), f32[8,56,128]{2,1,0:T(8,128)S(1)}, u32[]{:S(2)}, u32[]{:S(2)}) async-start(f32[8,56,128]{2,1,0:T(8,128)} %shard_map.125), calls=%async_computation.3 | async-start | bytes 458752 | tf_op jit(solution)/shard_map/all_to_all | solution.py:474

commit v6 on v4

--- a/solution.py
+++ b/solution.py
@@ -147,7 +147,7 @@
     lax.fori_loop(0, TOK // 16, square, 0)
     cols = pl.ds(pl.multiple_of(lax.axis_index("fsdp") // 8 * HALF, 128), HALF)
     prod_ref[...] = mm(x_ref[:, cols], w_ref[...], 1, 0)
-    gram_ref[...] = mm(w_ref[...], w_ref[...], 0, 0)
+    gram_ref[...] = mm(w_ref[:, 128:], w_ref[...], 0, 0)
 
 
 def local_kernel(
@@ -180,7 +180,7 @@
     w_ref[pl.ds(pl.multiple_of((1 - side) * HALF, 256), HALF), :] = w_far[...]
     cols = pl.ds(pl.multiple_of((1 - side) * HALF, 128), HALF)
     prod = prod_near[...] + mm(x_ref[:, cols], w_far[...], 1, 0)
-    gram = gram_near[...] + mm(w_far[...], w_far[...], 0, 0)
+    gram = gram_near[...] + mm(w_far[:, 128:], w_far[...], 0, 0)
     pre = prod[:, :128]
     x_up = prod[:, 128:]
     lane = lanes((TOK, 128))
@@ -188,7 +188,7 @@
     sig = 1.0 / (1.0 + jnp.exp(-pre))
     act_b = jnp.where(unit, pre * sig, 0.0).astype(bf16)
     act = act_b.astype(f32)
-    g_hi, g_lo = halves(gram[128:, :])
+    g_hi, g_lo = halves(gram)
     through = mm(act_b, g_hi, 1, 0) + mm(act_b, g_lo, 1, 0)
     m_left = pre + through[:, :128]
     m_up = x_up + through[:, 128:]
@@ -203,7 +203,7 @@
     weight = jnp.where(valid, loss_scale / count, 0.0)
     alpha = inv * weight
     beta = inv * inv * weight * score * (1.0 / D)
-    up_head = gram[R : R + 1, 128:] + gram[128 + R : 129 + R, 128:]
+    up_head = jnp.transpose(gram[:, :128])[R : R + 1] + gram[R : R + 1, 128:]
     back = alpha * up_head - beta * m_up
     pre_grad = back * sig * (1.0 + pre * (1.0 - sig))
     nab = -(act * beta)
@@ -400,7 +400,7 @@
         out_shape=(
             jax.ShapeDtypeStruct((HALF, 256), bf16),
             jax.ShapeDtypeStruct((TOK, 256), f32),
-            jax.ShapeDtypeStruct((256, 256), f32),
+            jax.ShapeDtypeStruct((128, 256), f32),
             jax.ShapeDtypeStruct((TOK, 128), f32),
         ),
         in_specs=[VMEM, VMEM, VMEM],

time: 153 us -> 153 us (level)
  no operation moved by 1% of the time
where the time goes in v6:
time: 153 us; the launch traced here: 150 us
  blocking collectives  71.1 us (46%)
  waiting for transfers between devices  28 us (18%)
  starting transfers between devices  27.5 us (18%)
  Pallas kernels  16.5 us (11%)
  local copies, waits for them, and re-layouts  2.87 us (2%)
  other arithmetic  2.2 us (1%)
  between operations  2.11 us (1%)
    all_to_all x1, blocking collectives, on_device(): lax.all_to_all(coded_terms, 'fsdp', 0, 0, axis_index_groups=parity, tiled...  30.5 us
    all_to_all x1, blocking collectives, on_device(): lax.all_to_all(packed, 'fsdp', 0, 0, axis_index_groups=along_y, tiled=True)  21.3 us
    all_to_all x1, blocking collectives, on_device(): lax.all_to_all(sums, 'cand', 0, 0, axis_index_groups=along_z, tiled=True)  19.3 us
    ppermute x1, waiting for transfers between devices, on_device(): got_b = lax.ppermute(send_b, 'fsdp', turn)  12.5 us
    all_to_all x1, waiting for transfers between devices, on_device(): lax.all_to_all(final, 'cand', 0, 0, axis_index_groups=along_z, tiled=True)  8.57 us
    pallas_call x1, Pallas kernels, on_device(): pl.pallas_call(local_kernel, out_shape=(jax.ShapeDtypeStruct((8, CUT + 16...  7.83 us
    pallas_call x1, Pallas kernels, on_device(): pl.pallas_call(near_kernel, out_shape=(jax.ShapeDtypeStruct((HALF, 256),...  5.26 us
    ppermute x1, starting transfers between devices, on_device(): beside = lax.ppermute(pieces, 'cand', sibling)  5.25 us
  transfers between devices with their start and end apart: 8, of which 6 were waited for; matrix products, arithmetic and copies ran while one was open for 0% of the time, Pallas kernels for 4%

profile of v6, /device:TPU:1, one launch (start us, length us, event | category | flops | bytes accessed | tf_op | source)
XLA Modules:
  0.0 150.3 jit_solution(7432092320038935039)
XLA Ops:
  0.6 0.7 fusion
  1.3 0.9 broadcast_select_fusion
  2.3 0.2 shard_map.119
  2.5 21.3 %all_to_all.20.mine_ref = bf16[8,224,128]{2,1,0:T(8,128)(2,1)S(1)} all-to-all(bf16[8,224,128]{2,1,0:T(8,128)(2,1)S(1)} %shard_map.119), channel_id=1, replica_groups={{0,2,4,6,8,10,12,14},{16,18,20,22,24,26,28,30},{1,3,5,7,9,11,13,15},{17..., dimensions={0} | all-to-all | bytes 917504 | tf_op jit(solution)/shard_map/all_to_all | solution.py:394
  23.7 5.1 %collective-permute-start = (bf16[8,224,128]{2,1,0:T(8,128)(2,1)S(1)}, bf16[8,224,128]{2,1,0:T(8,128)(2,1)S(1)}, u32[]{:S(2)}, u32[]{:S(2)}) collective-permute-start(bf16[8,224,128]{2,1,0:T(8,128)(2,1)S(1)} %all_to_all.20.mine_ref), channel_id=1, source_target_pairs={{0,32},{32,0},{64,96},{96,64},{128,160},{160,128},{192,224},{224,1... | collective-permute-start | bytes 1376264 | tf_op jit(solution)/shard_map/ppermute | solution.py:397
  28.9 4.7 %collective-permute-start.1 = (bf16[8,224,128]{2,1,0:T(8,128)(2,1)S(1)}, bf16[8,224,128]{2,1,0:T(8,128)(2,1)S(1)}, u32[]{:S(2)}, u32[]{:S(2)}) collective-permute-start(bf16[8,224,128]{2,1,0:T(8,128)(2,1)S(1)} %all_to_all.20.mine_ref), channel_id=1, source_target_pairs={{0,16},{2,18},{4,20},{6,22},{8,24},{10,26},{12,28},{14,30},{16,0},... | collective-permute-start | bytes 1376264 | tf_op jit(solution)/shard_map/ppermute | solution.py:396
  33.5 0.0 copy-start
  33.6 2.3 %copy-done = bf16[1,1,512,4608]{3,2,1,0:T(8,128)(2,1)S(1)} copy-done((bf16[1,1,512,4608]{3,2,1,0:T(8,128)(2,1)S(1)}, bf16[1,1,512,4608]{3,2,1,0:T(8,128)(2,1)}, u32[]{:S(2)}) %copy-start) | copy-done | bytes 4718616
  35.9 5.3 %shard_map.120 = (bf16[2304,256]{1,0:T(8,128)(2,1)S(1)}, f32[512,256]{1,0:T(8,128)S(1)}, f32[128,256]{1,0:T(8,128)S(1)}, f32[512,128]{1,0:T(8,128)S(1)}) custom-call(bf16[512,4608]{1,0:T(8,128)(2,1)S(1)} %bitcast.5, bf16[8,224,128]{2,1,0:T(8,128)(2,1)S(1)} %all_to_all.20.mine_ref, bf16[8,224,128]{2,1,0:T(8,128)(2,1)S(1)} %collective-permute-done.other_ref), custom_call_target="tpu_custom_call" | custom-call | tf_op jit(solution)/shard_map/pallas_call | solution.py:398
  41.2 3.3 %collective-permute-done.1.mine_ref = bf16[8,224,128]{2,1,0:T(8,128)(2,1)S(1)} collective-permute-done((bf16[8,224,128]{2,1,0:T(8,128)(2,1)S(1)}, bf16[8,224,128]{2,1,0:T(8,128)(2,1)S(1)}, u32[]{:S(2)}, u32[]{:S(2)}) %collective-permute-start.1) | collective-permute-done | bytes 458784 | tf_op jit(solution)/shard_map/ppermute | solution.py:396
  44.4 2.7 %collective-permute-start.2 = (bf16[8,224,128]{2,1,0:T(8,128)(2,1)S(1)}, bf16[8,224,128]{2,1,0:T(8,128)(2,1)S(1)}, u32[]{:S(2)}, u32[]{:S(2)}) collective-permute-start(bf16[8,224,128]{2,1,0:T(8,128)(2,1)S(1)} %collective-permute-done.1.mine_ref), channel_id=1, source_target_pairs={{0,32},{32,0},{64,96},{96,64},{128,160},{160,128},{192,224},{224,1... | collective-permute-start | bytes 1376264 | tf_op jit(solution)/shard_map/ppermute | solution.py:411
  48.4 0.1 collective-permute-done.2.other_ref
  48.5 7.8 %shard_map.121 = (s16[8,240,128]{2,1,0:T(8,128)(2,1)S(1)}, s16[8,224,128]{2,1,0:T(8,128)(2,1)S(1)}, f32[8,288,128]{2,1,0:T(8,128)S(1)}, f32[8,144,128]{2,1,0:T(8...) custom-call(s32[1,1]{1,0:T(1,128)S(6)} %copy.14.starts, s32[1,1]{1,0:T(1,128)S(6)} %copy.13.lengths, ...), custom_call_target="tpu_custom_call" | custom-call | tf_op jit(solution)/shard_map/pallas_call | solution.py:413
  56.4 2.2 %collective-permute-start.3 = (s16[8,240,128]{2,1,0:T(8,128)(2,1)S(1)}, s16[8,240,128]{2,1,0:T(8,128)(2,1)S(1)}, u32[]{:S(2)}, u32[]{:S(2)}) collective-permute-start(s16[8,240,128]{2,1,0:T(8,128)(2,1)S(1)} %get-tuple-element.27), channel_id=1, source_target_pairs={{0,2},{2,0},{4,6},{6,4},{8,10},{10,8},{12,14},{14,12},{16,18},{18,... | collective-permute-start | bytes 1474568 | tf_op jit(solution)/shard_map/ppermute | solution.py:433
  58.6 2.0 %collective-permute-start.4 = (s16[8,224,128]{2,1,0:T(8,128)(2,1)S(1)}, s16[8,224,128]{2,1,0:T(8,128)(2,1)S(1)}, u32[]{:S(2)}, u32[]{:S(2)}) collective-permute-start(s16[8,224,128]{2,1,0:T(8,128)(2,1)S(1)} %get-tuple-element.28), channel_id=1, source_target_pairs={{0,14},{2,4},{4,2},{6,8},{8,6},{10,12},{12,10},{14,0},{16,30},{18,... | collective-permute-start | bytes 1376264 | tf_op jit(solution)/shard_map/ppermute | solution.py:435
  60.6 12.5 %collective-permute-done.4.got_b = s16[8,224,128]{2,1,0:T(8,128)(2,1)S(1)} collective-permute-done((s16[8,224,128]{2,1,0:T(8,128)(2,1)S(1)}, s16[8,224,128]{2,1,0:T(8,128)(2,1)S(1)}, u32[]{:S(2)}, u32[]{:S(2)}) %collective-permute-start.4) | collective-permute-done | bytes 458784 | tf_op jit(solution)/shard_map/ppermute | solution.py:435
  73.1 0.6 shard_map.122
  73.7 0.0 copy-start.2
  73.8 30.5 %all_to_all.21.q_ref = s16[8,448,128]{2,1,0:T(8,128)(2,1)S(1)} all-to-all(s16[8,448,128]{2,1,0:T(8,128)(2,1)S(1)} %shard_map.122), channel_id=1, replica_groups={{0,4,8,12,16,20,24,28},{2,6,10,14,18,22,26,30},{1,5,9,13,17,21,25,29},{..., dimensions={0} | all-to-all | bytes 1835008 | tf_op jit(solution)/shard_map/all_to_all | solution.py:444
  104.2 0.8 shard_map.123
  105.1 19.3 %all_to_all.22.d_ref = f32[8,64,128]{2,1,0:T(8,128)S(1)} all-to-all(f32[8,64,128]{2,1,0:T(8,128)S(1)} %shard_map.123), channel_id=1, replica_groups={{0,64,128,192,256,320,384,448},{32,96,160,224,288,352,416,480},{1,65,12..., dimensions={0} | all-to-all | bytes 524288 | tf_op jit(solution)/shard_map/all_to_all | solution.py:453
  124.4 5.2 %collective-permute-start.5 = (f32[8,64,128]{2,1,0:T(8,128)S(1)}, f32[8,64,128]{2,1,0:T(8,128)S(1)}, u32[]{:S(2)}, u32[]{:S(2)}) collective-permute-start(f32[8,64,128]{2,1,0:T(8,128)S(1)} %all_to_all.22.d_ref), channel_id=1, source_target_pairs={{0,32},{32,0},{64,96},{96,64},{128,160},{160,128},{192,224},{224,1... | collective-permute-start | bytes 786440 | tf_op jit(solution)/shard_map/ppermute | solution.py:454
  129.7 1.1 collective-permute-done.5.o_ref
  130.8 0.2 shard_map.124
  131.0 2.2 %collective-permute-start.6 = (f32[56,128]{1,0:T(8,128)S(1)}, f32[56,128]{1,0:T(8,128)S(1)}, u32[]{:S(2)}, u32[]{:S(2)}) collective-permute-start(f32[56,128]{1,0:T(8,128)S(1)} %get-tuple-element.34.a_ref), channel_id=1, source_target_pairs={{0,1},{1,0},{2,3},{3,2},{4,5},{5,4},{6,7},{7,6},{8,9},{9,8},{10,11... | collective-permute-start | bytes 86024 | tf_op jit(solution)/shard_map/ppermute | solution.py:468
  133.3 2.4 %collective-permute-done.6.b_ref = f32[56,128]{1,0:T(8,128)S(1)} collective-permute-done((f32[56,128]{1,0:T(8,128)S(1)}, f32[56,128]{1,0:T(8,128)S(1)}, u32[]{:S(2)}, u32[]{:S(2)}) %collective-permute-start.6) | collective-permute-done | bytes 28704 | tf_op jit(solution)/shard_map/ppermute | solution.py:468
  135.7 0.7 shard_map.125
  136.4 3.4 %all-to-all-start.3 = ((f32[8,56,128]{2,1,0:T(8,128)}), f32[8,56,128]{2,1,0:T(8,128)S(1)}, u32[]{:S(2)}, u32[]{:S(2)}) async-start(f32[8,56,128]{2,1,0:T(8,128)} %shard_map.125), calls=%async_computation.3 | async-start | bytes 458752 | tf_op jit(solution)/shard_map/all_to_all | solution.py:469
  139.8 0.5 slice.9
  140.3 8.6 %all-to-all-done.3 = f32[8,56,128]{2,1,0:T(8,128)S(1)} async-done(((f32[8,56,128]{2,1,0:T(8,128)}), f32[8,56,128]{2,1,0:T(8,128)S(1)}, u32[]{:S(2)}, u32[]{:S(2)}) %all-to-all-start.3) | async-done | bytes 229408 | tf_op jit(solution)/shard_map/all_to_all | solution.py:469
  148.9 0.9 shard_map.126
  149.7 0.6 convert_multiply_fusion.2
  (12 shorter events, 0.0 us)
Async XLA Ops:
  23.7 9.8 %collective-permute-start = (bf16[8,224,128]{2,1,0:T(8,128)(2,1)S(1)}, bf16[8,224,128]{2,1,0:T(8,128)(2,1)S(1)}, u32[]{:S(2)}, u32[]{:S(2)}) collective-permute-start(bf16[8,224,128]{2,1,0:T(8,128)(2,1)S(1)} %all_to_all.20.mine_ref), channel_id=1, source_target_pairs={{0,32},{32,0},{64,96},{96,64},{128,160},{160,128},{192,224},{224,1... | collective-permute-start | bytes 1376264 | tf_op jit(solution)/shard_map/ppermute | solution.py:397
  28.9 15.5 %collective-permute-start.1 = (bf16[8,224,128]{2,1,0:T(8,128)(2,1)S(1)}, bf16[8,224,128]{2,1,0:T(8,128)(2,1)S(1)}, u32[]{:S(2)}, u32[]{:S(2)}) collective-permute-start(bf16[8,224,128]{2,1,0:T(8,128)(2,1)S(1)} %all_to_all.20.mine_ref), channel_id=1, source_target_pairs={{0,16},{2,18},{4,20},{6,22},{8,24},{10,26},{12,28},{14,30},{16,0},... | collective-permute-start | bytes 1376264 | tf_op jit(solution)/shard_map/ppermute | solution.py:396
  33.5 2.3 %copy-start = (bf16[1,1,512,4608]{3,2,1,0:T(8,128)(2,1)S(1)}, bf16[1,1,512,4608]{3,2,1,0:T(8,128)(2,1)}, u32[]{:S(2)}) copy-start(bf16[1,1,512,4608]{3,2,1,0:T(8,128)(2,1)} %param.8) | copy-start | bytes 14155780
  35.9 12.7 %copy-start.1 = (bf16[1,1,512,4608]{3,2,1,0:T(8,128)(2,1)S(1)}, bf16[1,1,512,4608]{3,2,1,0:T(8,128)(2,1)}, u32[]{:S(2)}) copy-start(bf16[1,1,512,4608]{3,2,1,0:T(8,128)(2,1)} %param.8) | copy-start | bytes 14155780
  44.4 4.1 %collective-permute-start.2 = (bf16[8,224,128]{2,1,0:T(8,128)(2,1)S(1)}, bf16[8,224,128]{2,1,0:T(8,128)(2,1)S(1)}, u32[]{:S(2)}, u32[]{:S(2)}) collective-permute-start(bf16[8,224,128]{2,1,0:T(8,128)(2,1)S(1)} %collective-permute-done.1.mine_ref), channel_id=1, source_target_pairs={{0,32},{32,0},{64,96},{96,64},{128,160},{160,128},{192,224},{224,1... | collective-permute-start | bytes 1376264 | tf_op jit(solution)/shard_map/ppermute | solution.py:411
  56.4 16.7 %collective-permute-start.3 = (s16[8,240,128]{2,1,0:T(8,128)(2,1)S(1)}, s16[8,240,128]{2,1,0:T(8,128)(2,1)S(1)}, u32[]{:S(2)}, u32[]{:S(2)}) collective-permute-start(s16[8,240,128]{2,1,0:T(8,128)(2,1)S(1)} %get-tuple-element.27), channel_id=1, source_target_pairs={{0,2},{2,0},{4,6},{6,4},{8,10},{10,8},{12,14},{14,12},{16,18},{18,... | collective-permute-start | bytes 1474568 | tf_op jit(solution)/shard_map/ppermute | solution.py:433
  58.6 14.5 %collective-permute-start.4 = (s16[8,224,128]{2,1,0:T(8,128)(2,1)S(1)}, s16[8,224,128]{2,1,0:T(8,128)(2,1)S(1)}, u32[]{:S(2)}, u32[]{:S(2)}) collective-permute-start(s16[8,224,128]{2,1,0:T(8,128)(2,1)S(1)} %get-tuple-element.28), channel_id=1, source_target_pairs={{0,14},{2,4},{4,2},{6,8},{8,6},{10,12},{12,10},{14,0},{16,30},{18,... | collective-permute-start | bytes 1376264 | tf_op jit(solution)/shard_map/ppermute | solution.py:435
  73.7 30.5 %copy-start.2 = (s32[1,16]{1,0:T(1,128)S(1)}, s32[1,16]{1,0:T(1,128)}, u32[]{:S(2)}) copy-start(s32[1,16]{1,0:T(1,128)} %ranking.1) | copy-start | bytes 196
  105.1 44.7 %copy-start.3 = (bf16[288]{0:T(512)(128)(2,1)S(1)}, bf16[288]{0:T(512)(128)(2,1)}, u32[]{:S(2)}) copy-start(bf16[288]{0:T(512)(128)(2,1)} %param.15) | copy-start | bytes 1732
  105.1 44.7 %copy-start.4 = (bf16[288]{0:T(512)(128)(2,1)S(1)}, bf16[288]{0:T(512)(128)(2,1)}, u32[]{:S(2)}) copy-start(bf16[288]{0:T(512)(128)(2,1)} %param.14) | copy-start | bytes 1732
  124.4 6.4 %collective-permute-start.5 = (f32[8,64,128]{2,1,0:T(8,128)S(1)}, f32[8,64,128]{2,1,0:T(8,128)S(1)}, u32[]{:S(2)}, u32[]{:S(2)}) collective-permute-start(f32[8,64,128]{2,1,0:T(8,128)S(1)} %all_to_all.22.d_ref), channel_id=1, source_target_pairs={{0,32},{32,0},{64,96},{96,64},{128,160},{160,128},{192,224},{224,1... | collective-permute-start | bytes 786440 | tf_op jit(solution)/shard_map/ppermute | solution.py:454
  131.0 4.6 %collective-permute-start.6 = (f32[56,128]{1,0:T(8,128)S(1)}, f32[56,128]{1,0:T(8,128)S(1)}, u32[]{:S(2)}, u32[]{:S(2)}) collective-permute-start(f32[56,128]{1,0:T(8,128)S(1)} %get-tuple-element.34.a_ref), channel_id=1, source_target_pairs={{0,1},{1,0},{2,3},{3,2},{4,5},{5,4},{6,7},{7,6},{8,9},{9,8},{10,11... | collective-permute-start | bytes 86024 | tf_op jit(solution)/shard_map/ppermute | solution.py:468
  136.4 12.5 %all-to-all-start.3 = ((f32[8,56,128]{2,1,0:T(8,128)}), f32[8,56,128]{2,1,0:T(8,128)S(1)}, u32[]{:S(2)}, u32[]{:S(2)}) async-start(f32[8,56,128]{2,1,0:T(8,128)} %shard_map.125), calls=%async_computation.3 | async-start | bytes 458752 | tf_op jit(solution)/shard_map/all_to_all | solution.py:469
